TPU v7x, 256 devices: a whole 4x4x8 slice. The times are simulated.
256 devices in a mesh: section: 8 (over x, y_hi), replica: 16 (over z, core), tensor: 2 (over y_lo).
Axes of the slice: x: 4, y: 4 (y_hi: 2, y_lo: 2; y = y_hi * 2 + y_lo), z: 8, core: 2. Of those that a mesh axis runs over, the one named last changes fastest.
Arguments:
- fresh: bfloat16 [8, 16, 16, 16, 2560], P('section', 'replica', None, None, 'tensor'), may hold values from -6 to 6
- counts: int32 [8, 16], P('section', 'replica'), may hold values from 4 to 16, as said below
- wiring: int32 [8, 16, 16, 1], P('section', 'replica'), may hold values from 0 to 15; in each aligned block of 16 rows (0 to 15, 16 to 31, ..., all dimensions but the last counted through in order) at most 2 rows name the same one
- weights: bfloat16 [8, 2560, 2560], P('section', 'tensor'), may hold values from -0.125 to 0.125
- kept: bfloat16 [8, 16, 32, 16, 2560], P('section', 'replica', None, None, 'tensor'), may hold values from -6 to 6
- upstream: bfloat16 [8, 16, 32, 16, 2560], P('section', 'replica', None, None, 'tensor'), may hold values from -6 to 6
Outputs:
- arrived: bfloat16 [8, 16, 32, 16, 2560], P('section', 'replica', None, None, 'tensor')
- returned: bfloat16 [8, 16, 16, 16, 2560], P('section', 'replica', None, None, 'tensor')
- weight_grad: float32 [8, 2560, 2560], P('section', ('tensor', 'replica'))
Inputs may be any that keep to these rules, and one draw needn't show every extreme that they name: `counts`: each section has a replica with all 16 slots live and one with 4; every count is 16, 8 or 4. `wiring`: the slots of one replica name each next-section replica at most 2 times.
All inputs are finite; a program needn't handle non-finite values.
Results may differ from a plain program's by a relative error of at most 0.0034.
Values may be sent and summed in bfloat16 or wider, within the bound.
No kernel may reach another device: no remote copies, remote signals or barrier semaphores. Data moves between devices by JAX's collectives and lax.ppermute only.
A program may use at most 128 MiB of HBM per device.

v0:
```python
import jax
import jax.numpy as jnp
from jax import lax
from jax.sharding import PartitionSpec as P


def from_behind(block, axis, distance):
    devices = range(lax.axis_size(axis))
    route = [(i - distance, i) for i in devices if i - distance in devices]
    return lax.ppermute(block, axis, route)


def local(fresh, counts, wiring, weights, kept, upstream):
    replicas = lax.axis_size("replica")
    slot_count = fresh.shape[2]
    row_count = fresh.shape[3]
    local_width = fresh.shape[4]
    recv_count = kept.shape[2]
    pair_cap = recv_count // replicas
    weight = weights[0]
    slot_index = jnp.arange(slot_count)
    target = wiring[0, 0, :, 0]
    same_target = target[:, None] == target[None, :]
    earlier = slot_index[None, :] < slot_index[:, None]
    pair_rank = jnp.sum(same_target & earlier, axis=1)
    buffer_slot = target * pair_cap + pair_rank
    selector = (buffer_slot[:, None] == jnp.arange(recv_count)[None, :]).astype(jnp.bfloat16)
    live_slots = (slot_index < counts[0, 0]).astype(jnp.float32)
    inputs = fresh[0, 0].reshape(slot_count * row_count, local_width)
    stored = kept[0, 0].reshape(recv_count * row_count, local_width)
    forward_part = jnp.dot(inputs, weight, preferred_element_type=jnp.float32)
    backward_part = jnp.dot(stored, weight, preferred_element_type=jnp.float32)
    forward_z, backward_z = (
        lax.psum_scatter(forward_part, "tensor", scatter_dimension=1, tiled=True),
        lax.psum_scatter(backward_part, "tensor", scatter_dimension=1, tiled=True),
    )
    live_rows = jnp.repeat(live_slots, row_count)[:, None]
    outputs = ((inputs.astype(jnp.float32) + jax.nn.silu(forward_z)) * live_rows).astype(
        jnp.bfloat16
    )
    outputs = outputs.reshape(slot_count, row_count * local_width)
    packed = lax.dot_general(
        selector, outputs, (((0,), (0,)), ((), ())), preferred_element_type=jnp.float32
    )
    packed = packed.astype(jnp.bfloat16).reshape(replicas, pair_cap, row_count * local_width)
    flags = (
        jnp.dot(live_slots, selector.astype(jnp.float32))
        .reshape(replicas, pair_cap)
        .astype(jnp.bfloat16)
    )
    arrived_buf, live_marks = (
        lax.all_to_all(packed, "replica", split_axis=0, concat_axis=0, tiled=True),
        lax.all_to_all(flags, "replica", split_axis=0, concat_axis=0, tiled=True),
    )
    arrived_buf, live_marks = from_behind((arrived_buf, live_marks), "section", 1)
    arrived = arrived_buf.reshape(1, 1, recv_count, row_count, local_width)
    mask_rows = jnp.repeat(live_marks.reshape(recv_count).astype(jnp.float32), row_count)[:, None]
    grads_in = upstream[0, 0].reshape(recv_count * row_count, local_width).astype(jnp.float32)
    sigmoid_z = jax.nn.sigmoid(backward_z)
    z_slope = sigmoid_z * (1.0 + backward_z * (1.0 - sigmoid_z))
    gate_grad = (grads_in * z_slope * mask_rows).astype(jnp.bfloat16)
    gate_full = lax.all_gather(gate_grad, "tensor", axis=1, tiled=True)
    back_terms = lax.dot_general(
        gate_full, weight, (((1,), (1,)), ((), ())), preferred_element_type=jnp.float32
    )
    input_grad = ((grads_in + back_terms) * mask_rows).astype(jnp.bfloat16)
    input_grad = input_grad.reshape(replicas, pair_cap, row_count * local_width)
    weight_grad = lax.psum_scatter(
        lax.dot_general(
            stored, gate_full, (((0,), (0,)), ((), ())), preferred_element_type=jnp.float32
        ),
        "replica",
        scatter_dimension=0,
        tiled=True,
    )
    back_buf = lax.all_to_all(input_grad, "replica", split_axis=0, concat_axis=0, tiled=True)
    back_buf = from_behind(back_buf, "section", -1)
    back_flat = back_buf.reshape(recv_count, row_count * local_width)
    returned = jnp.dot(selector, back_flat, preferred_element_type=jnp.float32).astype(jnp.bfloat16)
    returned = returned.reshape(1, 1, slot_count, row_count, local_width)
    return (arrived, returned, weight_grad[None])


def solution(mesh):
    placed = (
        P("section", "replica", None, None, "tensor"),
        P("section", "replica"),
        P("section", "replica", None, None),
        P("section", "tensor", None),
        P("section", "replica", None, None, "tensor"),
        P("section", "replica", None, None, "tensor"),
    )
    return jax.shard_map(
        local,
        mesh=mesh,
        in_specs=placed,
        out_specs=(
            P("section", "replica", None, None, "tensor"),
            P("section", "replica", None, None, "tensor"),
            P("section", ("tensor", "replica"), None),
        ),
        check_vma=False,
    )
```

profile of v0, /device:TPU:2, one launch (start us, length us, event | category | flops | bytes accessed | tf_op | source)
XLA Modules:
  0.0 334.8 jit_solution(15073978647920094325)
XLA Ops:
  8.5 8.1 %fusion.2 = f32[512,2560]{1,0:T(8,128)} fusion(bf16[512,1280]{1,0:T(8,128)(2,1)S(1)} %bitcast.46, bf16[1,1280,2560]{2,1,0:T(8,128)(2,1)} %param.9), kind=kOutput, calls=%fused_computation.5 | convolution fusion | flops 3355443200 | bytes 13107200 | tf_op jit(solution)/shard_map/dot_general | solution.py:32
  17.9 15.9 %all_to_all.19 = bf16[16,1,2]{2,1,0:T(2,128)(2,1)S(1)} all-to-all(bf16[16,1,2]{2,1,0:T(2,128)(2,1)S(1)} %convert_element_type.67), channel_id=1, replica_groups=mesh['section'=8,'replica'=16,'tensor'=2] {'replica'}, dimensions={0} | all-to-all | bytes 128 | tf_op jit(solution)/shard_map/all_to_all | solution.py:53
  33.9 5.1 %collective-permute-start.1 = (bf16[16,2]{0,1:T(2,128)(2,1)S(1)}, bf16[16,2]{0,1:T(2,128)(2,1)S(1)}, u32[]{:S(2)}, u32[]{:S(2)}) collective-permute-start(bf16[16,2]{0,1:T(2,128)(2,1)S(1)} %bitcast.53), channel_id=1, source_target_pairs={{0,32},{32,64},{64,96},{96,128},{128,160},{160,192},{192,224},{1,3... | collective-permute-start | bytes 200 | tf_op jit(solution)/shard_map/ppermute | solution.py:10
  39.0 2.7 collective-permute-done.1
  42.1 48.4 %reduce-scatter.8.cloned.1.call-done = f32[512,1280]{1,0:T(8,128)} async-done(((f32[512,2560]{1,0:T(8,128)}), f32[512,1280]{1,0:T(8,128)}) %reduce-scatter.8.cloned.1.call-update) | async-done | bytes 2621456 | tf_op jit(solution)/shard_map/reduce_scatter | solution.py:35
  90.5 3.9 %fusion.16 = bf16[512,1280]{1,0:T(8,128)(2,1)} fusion(f32[512,1280]{1,0:T(8,128)} %reduce-scatter.8.cloned.1.call-done, f32[512]{0:T(512)S(1)} %mul.54, bf16[1,1,32,16,1280]{4,3,2,1,0:T(8,128)(2,1)S(1)} %copy-done.2), kind=kLoop, calls=%fused_computation.14 | loop fusion | flops 7208960 | bytes 5244928 | tf_op jit(solution)/shard_map/convert_element_type | solution.py:61
  94.5 6.2 %fusion.4 = f32[256,2560]{1,0:T(8,128)} fusion(bf16[256,1280]{1,0:T(8,128)(2,1)S(1)} %bitcast.52, bf16[1,1280,2560]{2,1,0:T(8,128)(2,1)} %param.9), kind=kOutput, calls=%fused_computation.7 | convolution fusion | flops 1677721600 | bytes 9830400 | tf_op jit(solution)/shard_map/dot_general | solution.py:31
  100.8 38.9 %all-gather.2.cloned.1.call-done = bf16[512,2560]{1,0:T(8,128)(2,1)} async-done(((bf16[512,1280]{1,0:T(8,128)(2,1)}), bf16[512,2560]{1,0:T(8,128)(2,1)}) %all-gather.2.cloned.1.call-update) | async-done | bytes 2621456 | tf_op jit(solution)/shard_map/all_gather | solution.py:62
  139.8 9.1 %convolution_bitcast_fusion = f32[1280,2560]{0,1:T(8,128)} fusion(bf16[512,2560]{1,0:T(8,128)(2,1)} %all-gather.2.cloned.1.call-done, bf16[512,1280]{1,0:T(8,128)(2,1)S(1)} %bitcast.47), kind=kOutput, calls=%fused_computation.2 | convolution fusion | flops 3355443200 | bytes 17039360 | tf_op jit(solution)/shard_map/dot_general | solution.py:69
  148.9 14.0 %copy.23 = f32[1280,2560]{1,0:T(8,128)} copy(f32[1280,2560]{0,1:T(8,128)} %convolution_bitcast_fusion) | data formatting | bytes 26214400
  163.1 23.1 %reduce-scatter.6.cloned.1.call-done = f32[256,1280]{1,0:T(8,128)} async-done(((f32[256,2560]{1,0:T(8,128)}), f32[256,1280]{1,0:T(8,128)}) %reduce-scatter.6.cloned.1.call-update) | async-done | bytes 1310736 | tf_op jit(solution)/shard_map/reduce_scatter | solution.py:34
  186.1 1.8 multiply_convert_fusion
  188.8 1.7 reshape.56
  190.5 7.1 %all-to-all-start = ((bf16[16,2,20480]{2,1,0:T(2,128)(2,1)}), bf16[16,2,20480]{2,1,0:T(2,128)(2,1)S(1)}, u32[]{:S(2)}, u32[]{:S(2)}) async-start(bf16[16,2,20480]{2,1,0:T(2,128)(2,1)} %reshape.56), calls=%async_computation.1 | async-start | bytes 2621440 | tf_op jit(solution)/shard_map/all_to_all | solution.py:52
  197.7 8.1 %fusion.12 = bf16[512,1280]{1,0:T(8,128)(2,1)S(1)} fusion(bf16[512,2560]{1,0:T(8,128)(2,1)} %all-gather.2.cloned.1.call-done, bf16[1,1280,2560]{2,1,0:T(8,128)(2,1)} %param.9, bf16[512,1280]{1,0:T(8,128)(2,1)} %bitcast.50, f32[512]{0:T(512)S(1)} %mul.54), kind=kOutput, calls=%fused_computation.12 | convolution fusion | flops 3358064640 | bytes 11798528 | tf_op jit(solution)/shard_map/dot_general | solution.py:63
  207.0 27.8 %all-to-all-done = bf16[16,2,20480]{2,1,0:T(2,128)(2,1)S(1)} async-done(((bf16[16,2,20480]{2,1,0:T(2,128)(2,1)}), bf16[16,2,20480]{2,1,0:T(2,128)(2,1)S(1)}, u32[]{:S(2)}, u32[]{:S(2)}) %all-to-all-start) | async-done | bytes 1310752 | tf_op jit(solution)/shard_map/all_to_all | solution.py:52
  234.7 6.4 %all-to-all-start.2 = ((bf16[16,2,20480]{2,1,0:T(2,128)(2,1)}), bf16[16,2,20480]{2,1,0:T(2,128)(2,1)S(1)}, u32[]{:S(2)}, u32[]{:S(2)}) async-start(bf16[16,2,20480]{2,1,0:T(2,128)(2,1)} %reshape.58), calls=%async_computation.4 | async-start | bytes 2621440 | tf_op jit(solution)/shard_map/all_to_all | solution.py:76
  241.1 4.6 %collective-permute-start = (bf16[16,2,20480]{2,1,0:T(2,128)(2,1)S(1)}, bf16[16,2,20480]{2,1,0:T(2,128)(2,1)}, u32[]{:S(2)}, u32[]{:S(2)}) collective-permute-start(bf16[16,2,20480]{2,1,0:T(2,128)(2,1)S(1)} %all-to-all-done), channel_id=1, source_target_pairs={{0,32},{32,64},{64,96},{96,128},{128,160},{160,192},{192,224},{1,3... | collective-permute-start | bytes 3932168 | tf_op jit(solution)/shard_map/ppermute | solution.py:10
  245.8 34.2 %all-to-all-done.2 = bf16[16,2,20480]{2,1,0:T(2,128)(2,1)S(1)} async-done(((bf16[16,2,20480]{2,1,0:T(2,128)(2,1)}), bf16[16,2,20480]{2,1,0:T(2,128)(2,1)S(1)}, u32[]{:S(2)}, u32[]{:S(2)}) %all-to-all-start.2) | async-done | bytes 1310752 | tf_op jit(solution)/shard_map/all_to_all | solution.py:76
  280.0 4.6 %collective-permute-start.2 = (bf16[16,2,20480]{2,1,0:T(2,128)(2,1)S(1)}, bf16[16,2,20480]{2,1,0:T(2,128)(2,1)}, u32[]{:S(2)}, u32[]{:S(2)}) collective-permute-start(bf16[16,2,20480]{2,1,0:T(2,128)(2,1)S(1)} %all-to-all-done.2), channel_id=1, source_target_pairs={{32,0},{64,32},{96,64},{128,96},{160,128},{192,160},{224,192},{33,... | collective-permute-start | bytes 3932168 | tf_op jit(solution)/shard_map/ppermute | solution.py:10
  284.7 4.5 %reshape.57 = bf16[1,1,32,16,1280]{4,3,2,1,0:T(8,128)(2,1)} reshape(bf16[16,2,20480]{2,1,0:T(2,128)(2,1)} %collective-permute-done) | data formatting | bytes 2621440 | tf_op jit(solution)/shard_map/reshape | solution.py:56
  289.2 25.8 %collective-permute-done.2 = bf16[16,2,20480]{2,1,0:T(2,128)(2,1)} collective-permute-done((bf16[16,2,20480]{2,1,0:T(2,128)(2,1)S(1)}, bf16[16,2,20480]{2,1,0:T(2,128)(2,1)}, u32[]{:S(2)}, u32[]{:S(2)}) %collective-permute-start.2) | collective-permute-done | bytes 1310752 | tf_op jit(solution)/shard_map/ppermute | solution.py:10
  315.0 1.6 reshape.59
  318.0 7.4 %reduce-scatter.10.cloned.1.call-done = f32[80,2560]{1,0:T(8,128)} async-done(((f32[1280,2560]{1,0:T(8,128)}), f32[80,2560]{1,0:T(8,128)}) %reduce-scatter.10.cloned.1.call-update) | async-done | bytes 819216
  (38 shorter events, 8.9 us)
Async XLA Ops:
  7.2 1.3 copy-start
  7.2 83.3 %reduce-scatter.8.cloned.1.call-start = ((), (), s32[]{:S(2)}) async-start(), calls=%async_computation.7 | async-start | bytes 7864320 | tf_op jit(solution)/shard_map/reduce_scatter | solution.py:35
  16.6 0.8 copy-start.4
  16.6 73.9 %copy-start.2 = (bf16[1,1,32,16,1280]{4,3,2,1,0:T(8,128)(2,1)S(1)}, bf16[1,1,32,16,1280]{4,3,2,1,0:T(8,128)(2,1)}, u32[]{:S(2)}) copy-start(bf16[1,1,32,16,1280]{4,3,2,1,0:T(8,128)(2,1)} %param.11) | copy-start | bytes 3932164
  16.6 123.2 %all-gather.2.cloned.1.call-start = ((), (), s32[]{:S(2)}) async-start(), calls=%async_computation.8 | async-start | bytes 3932160 | tf_op jit(solution)/shard_map/all_gather | solution.py:62
  33.9 7.8 %collective-permute-start.1 = (bf16[16,2]{0,1:T(2,128)(2,1)S(1)}, bf16[16,2]{0,1:T(2,128)(2,1)S(1)}, u32[]{:S(2)}, u32[]{:S(2)}) collective-permute-start(bf16[16,2]{0,1:T(2,128)(2,1)S(1)} %bitcast.53), channel_id=1, source_target_pairs={{0,32},{32,64},{64,96},{96,128},{128,160},{160,192},{192,224},{1,3... | collective-permute-start | bytes 200 | tf_op jit(solution)/shard_map/ppermute | solution.py:10
  42.1 52.4 %copy-start.3 = (bf16[1,1,16,16,1280]{4,3,2,1,0:T(8,128)(2,1)S(1)}, bf16[1,1,16,16,1280]{4,3,2,1,0:T(8,128)(2,1)}, u32[]{:S(2)}) copy-start(bf16[1,1,16,16,1280]{4,3,2,1,0:T(8,128)(2,1)} %param.6) | copy-start | bytes 1966084
  94.5 91.7 %reduce-scatter.6.cloned.1.call-start = ((), (), s32[]{:S(2)}) async-start(), calls=%async_computation.6 | async-start | bytes 3932160 | tf_op jit(solution)/shard_map/reduce_scatter | solution.py:34
  100.8 224.6 %reduce-scatter.10.cloned.1.call-start = ((), (), s32[]{:S(2)}) async-start(), calls=%async_computation.9 | async-start | bytes 13926400
  190.5 44.2 %all-to-all-start = ((bf16[16,2,20480]{2,1,0:T(2,128)(2,1)}), bf16[16,2,20480]{2,1,0:T(2,128)(2,1)S(1)}, u32[]{:S(2)}, u32[]{:S(2)}) async-start(bf16[16,2,20480]{2,1,0:T(2,128)(2,1)} %reshape.56), calls=%async_computation.1 | async-start | bytes 2621440 | tf_op jit(solution)/shard_map/all_to_all | solution.py:52
  234.7 45.3 %all-to-all-start.2 = ((bf16[16,2,20480]{2,1,0:T(2,128)(2,1)}), bf16[16,2,20480]{2,1,0:T(2,128)(2,1)S(1)}, u32[]{:S(2)}, u32[]{:S(2)}) async-start(bf16[16,2,20480]{2,1,0:T(2,128)(2,1)} %reshape.58), calls=%async_computation.4 | async-start | bytes 2621440 | tf_op jit(solution)/shard_map/all_to_all | solution.py:76
  241.1 43.5 %collective-permute-start = (bf16[16,2,20480]{2,1,0:T(2,128)(2,1)S(1)}, bf16[16,2,20480]{2,1,0:T(2,128)(2,1)}, u32[]{:S(2)}, u32[]{:S(2)}) collective-permute-start(bf16[16,2,20480]{2,1,0:T(2,128)(2,1)S(1)} %all-to-all-done), channel_id=1, source_target_pairs={{0,32},{32,64},{64,96},{96,128},{128,160},{160,192},{192,224},{1,3... | collective-permute-start | bytes 3932168 | tf_op jit(solution)/shard_map/ppermute | solution.py:10
  280.0 35.0 %collective-permute-start.2 = (bf16[16,2,20480]{2,1,0:T(2,128)(2,1)S(1)}, bf16[16,2,20480]{2,1,0:T(2,128)(2,1)}, u32[]{:S(2)}, u32[]{:S(2)}) collective-permute-start(bf16[16,2,20480]{2,1,0:T(2,128)(2,1)S(1)} %all-to-all-done.2), channel_id=1, source_target_pairs={{32,0},{64,32},{96,64},{128,96},{160,128},{192,160},{224,192},{33,... | collective-permute-start | bytes 3932168 | tf_op jit(solution)/shard_map/ppermute | solution.py:10
  317.0 11.2 %copy-start.1 = (bf16[1,1,32,16,1280]{4,3,2,1,0:T(8,128)(2,1)S(1)}, bf16[1,1,32,16,1280]{4,3,2,1,0:T(8,128)(2,1)}, u32[]{:S(2)}) copy-start(bf16[1,1,32,16,1280]{4,3,2,1,0:T(8,128)(2,1)} %param.10) | copy-start | bytes 3932164
Sparse Core Ops, SparseCore 0:
  16.7 73.7 reduce-scatter.7
  94.6 45.1 all-gather.1
  142.4 43.6 reduce-scatter.5
  188.6 136.8 reduce-scatter.9
where the time goes:
time: 336 us; the launch traced here: 335 us
  waiting for transfers between devices  208 us (62%)
  matrix products  32.7 us (10%)
  local copies, waits for them, and re-layouts  29.2 us (9%)
  starting transfers between devices  28.1 us (8%)
  blocking collectives  15.9 us (5%)
  between operations  14.6 us (4%)
  other arithmetic  5.9 us (2%)
    reduce_scatter x1, waiting for transfers between devices, local(): lax.psum_scatter(backward_part, 'tensor', scatter_dimension=1, tiled=True)  48.4 us
    all_gather x1, waiting for transfers between devices, local(): gate_full = lax.all_gather(gate_grad, 'tensor', axis=1, tiled=True)  38.9 us
    all_to_all x1, waiting for transfers between devices, local(): lax.all_to_all(input_grad, 'replica', split_axis=0, concat_axis=0, tiled=...  34.2 us
    ppermute x3, waiting for transfers between devices, from_behind(): return lax.ppermute(block, axis, route)  28.5 us
    all_to_all x1, waiting for transfers between devices, local(): lax.all_to_all(packed, 'replica', split_axis=0, concat_axis=0, tiled=True)  27.8 us
    reduce_scatter x1, waiting for transfers between devices, local(): lax.psum_scatter(forward_part, 'tensor', scatter_dimension=1, tiled=True)  23.1 us
    unnamed x14, local copies, waits for them, and re-layouts  19.1 us
    all_to_all x1, blocking collectives, local(): lax.all_to_all(flags, 'replica', split_axis=0, concat_axis=0, tiled=True)  15.9 us
  transfers between devices with their start and end apart: 9, of which 8 were waited for; matrix products, arithmetic and copies ran while one was open for 15% of the time, Pallas kernels for 0%

commit v1 on v0

v1 whole, which is shorter than its diff:
```python
import jax
import jax.numpy as jnp
from jax import lax
from jax.experimental import pallas as pl
from jax.experimental.pallas import tpu as pltpu
from jax.sharding import PartitionSpec as P

Z_SCALE = 64.0
Z_BACK = 1.0 / 64.0
TILE = 256
VMEM_BYTES = 40 * 1024 * 1024


def shift(block, axis, distance):
    devices = range(lax.axis_size(axis))
    route = [(i, i + distance) for i in devices if i + distance in devices]
    return lax.ppermute(block, axis, route)


def swap_tensor(block):
    return lax.ppermute(block, "tensor", [(0, 1), (1, 0)])


def swap_core(block):
    return lax.ppermute(block, "replica", [(r, r ^ 1) for r in range(lax.axis_size("replica"))])


def round_chips(block, distance):
    size = lax.axis_size("replica")
    return lax.ppermute(block, "replica", [(r, (r + 2 * distance) % size) for r in range(size)])


def params():
    return pltpu.CompilerParams(vmem_limit_bytes=VMEM_BYTES)


def cost(flops, moved):
    return pl.CostEstimate(flops=flops, bytes_accessed=moved, transcendentals=0)


def project_body(half_ref, x_ref, w_ref, o_ref):
    o_ref[...] = jnp.dot(x_ref[...], w_ref[...], preferred_element_type=jnp.float32)


def project(x, weight, half):
    rows, depth = x.shape
    width = weight.shape[1] // 2
    tiles = width // TILE
    return pl.pallas_call(
        project_body,
        grid_spec=pltpu.PrefetchScalarGridSpec(
            num_scalar_prefetch=1,
            grid=(tiles,),
            in_specs=[
                pl.BlockSpec((rows, depth), lambda j, h: (0, 0)),
                pl.BlockSpec((depth, TILE), lambda j, h: (0, h[0] * tiles + j)),
            ],
            out_specs=pl.BlockSpec((rows, TILE), lambda j, h: (0, j)),
        ),
        out_shape=jax.ShapeDtypeStruct((rows, width), jnp.float32),
        compiler_params=params(),
        cost_estimate=cost(2 * rows * depth * width, 2 * depth * width + 4 * rows * width),
    )(half, x, weight)


def back_body(half_ref, own_ref, nbr_ref, wo_ref, wn_ref, up_ref, mask_ref, o_ref):
    dims = (((1,), (1,)), ((), ()))
    terms = lax.dot_general(own_ref[...], wo_ref[...], dims, preferred_element_type=jnp.float32)
    terms += lax.dot_general(nbr_ref[...], wn_ref[...], dims, preferred_element_type=jnp.float32)
    o_ref[...] = ((up_ref[...].astype(jnp.float32) + terms) * mask_ref[...]).astype(jnp.bfloat16)


def back_project(own, nbr, weight, half, up, mask):
    rows, depth = own.shape
    width = weight.shape[0]
    return pl.pallas_call(
        back_body,
        grid_spec=pltpu.PrefetchScalarGridSpec(
            num_scalar_prefetch=1,
            grid=(width // TILE,),
            in_specs=[
                pl.BlockSpec((rows, depth), lambda j, h: (0, 0)),
                pl.BlockSpec((rows, depth), lambda j, h: (0, 0)),
                pl.BlockSpec((TILE, depth), lambda j, h: (j, h[0])),
                pl.BlockSpec((TILE, depth), lambda j, h: (j, 1 - h[0])),
                pl.BlockSpec((rows, TILE), lambda j, h: (0, j)),
                pl.BlockSpec((rows, 1), lambda j, h: (0, 0)),
            ],
            out_specs=pl.BlockSpec((rows, TILE), lambda j, h: (0, j)),
        ),
        out_shape=jax.ShapeDtypeStruct((rows, width), jnp.bfloat16),
        compiler_params=params(),
        cost_estimate=cost(4 * rows * depth * width, 4 * depth * width + 4 * rows * width),
    )(half, own, nbr, weight, weight, up, mask)


def outer_body(other_ref, mine_ref, ga_ref, gb_ref, send_ref, keep_ref):
    rows = ga_ref.shape[0]
    for lhs, out in ((other_ref, send_ref), (mine_ref, keep_ref)):
        out[...] = jnp.dot(lhs[:, :rows], ga_ref[...], preferred_element_type=jnp.float32) + jnp.dot(
            lhs[:, rows:], gb_ref[...], preferred_element_type=jnp.float32
        )


def outer_sum(other, mine, gate_a, gate_b):
    depth, rows = other.shape
    width = gate_a.shape[1]
    part = gate_a.shape[0]
    out = jax.ShapeDtypeStruct((depth, width), jnp.float32)
    return pl.pallas_call(
        outer_body,
        grid=(width // TILE,),
        in_specs=[
            pl.BlockSpec((depth, rows), lambda j: (0, 0)),
            pl.BlockSpec((depth, rows), lambda j: (0, 0)),
            pl.BlockSpec((part, TILE), lambda j: (0, j)),
            pl.BlockSpec((part, TILE), lambda j: (0, j)),
        ],
        out_specs=[pl.BlockSpec((depth, TILE), lambda j: (0, j))] * 2,
        out_shape=[out, out],
        compiler_params=params(),
        cost_estimate=cost(4 * rows * depth * width, 8 * depth * width),
    )(other, mine, gate_a, gate_b)


def pick_body(index_ref, x_ref, o_ref):
    def step(i, carry):
        source = index_ref[i]
        block = x_ref[jnp.maximum(source, 0)]
        o_ref[i] = jnp.where(source >= 0, block, jnp.zeros_like(block))
        return carry

    lax.fori_loop(0, o_ref.shape[0], step, 0)


def pick(index, x):
    count = index.shape[0]
    return pl.pallas_call(
        pick_body,
        in_specs=[
            pl.BlockSpec(memory_space=pltpu.SMEM),
            pl.BlockSpec(memory_space=pltpu.VMEM),
        ],
        out_specs=pl.BlockSpec(memory_space=pltpu.VMEM),
        out_shape=jax.ShapeDtypeStruct((count,) + x.shape[1:], x.dtype),
        compiler_params=params(),
        cost_estimate=cost(0, 2 * 2 * count * x.shape[1] * x.shape[2]),
    )(index, x)


def ring_sum(keep, send, scale):
    chips = lax.axis_size("replica") // 2
    me = lax.axis_index("replica") // 2
    got = swap_core(send)

    def term(offset):
        at = (me + offset + chips) % chips
        first = lax.dynamic_index_in_dim(keep, at, 0, keepdims=False)
        return (first + lax.dynamic_index_in_dim(got, at, 0, keepdims=False)) * scale

    down = up = None
    far = chips // 2
    for k in range(far, 0, -1):
        s = term(-k)
        s = s if down is None else s + down.astype(jnp.float32)
        down = round_chips(s.astype(jnp.float16), -1)
        if k < far:
            s = term(k)
            s = s if up is None else s + up.astype(jnp.float32)
            up = round_chips(s.astype(jnp.float16), 1)
    total = term(0) + down.astype(jnp.float32) + up.astype(jnp.float32)
    return total * (1.0 / scale)


def local(fresh, counts, wiring, weights, kept, upstream):
    replicas = lax.axis_size("replica")
    chips = replicas // 2
    slots, tokens, width = fresh.shape[2:]
    recv = kept.shape[2]
    cap = recv // replicas
    cut = tokens // 2
    weight = weights[0]
    own = lax.axis_index("tensor").astype(jnp.int32)[None]
    nbr = 1 - own
    core = lax.axis_index("replica") % 2

    plan = jnp.concatenate([wiring[0, 0, :, 0], counts[0]])[None]
    plan = shift(plan, "section", 1)[0]
    target, count = plan[:slots], plan[slots]
    slot = jnp.arange(slots)
    same = target[:, None] == target[None, :]
    rank = jnp.sum(same & (slot[None, :] < slot[:, None]), axis=1).astype(jnp.int32)
    place = target * cap + rank
    hit = (place[None, :] == jnp.arange(recv)[:, None]) & (slot < count)[None, :]
    source = (jnp.sum(jnp.where(hit, slot[None, :] + 1, 0), axis=1) - 1).astype(jnp.int32)
    flags = jnp.any(hit, axis=1).astype(jnp.bfloat16).reshape(replicas, cap)
    tops = jnp.stack([jnp.max(jnp.abs(kept)), jnp.max(jnp.abs(upstream))])
    tops = jnp.broadcast_to(tops[None], (replicas, 2))
    told = lax.all_to_all(
        jnp.concatenate([flags, tops], axis=1), "replica", split_axis=0, concat_axis=0, tiled=True
    ).astype(jnp.float32)
    marks = told[:, :cap].reshape(recv)
    terms = 1.11 * replicas * recv * tokens
    top_kept, top_own = jnp.max(told[:, cap]), jnp.max(told[:, cap + 1])
    top_nbr = swap_tensor(top_own[None])[0]
    scale_own = 60000.0 / (terms * jnp.maximum(top_kept * top_own, 1e-25))
    scale_nbr = 60000.0 / (terms * jnp.maximum(top_kept * top_nbr, 1e-25))
    mask = jnp.broadcast_to(marks[:, None], (recv, cut)).reshape(recv * cut, 1)

    inputs = fresh[0, 0].reshape(slots * tokens, width)
    away = (project(inputs, weight, nbr) * Z_SCALE).astype(jnp.float16)
    forward_away = swap_tensor(away)
    halves = lambda v: [
        v[0, 0, :, h * cut : (h + 1) * cut].reshape(recv * cut, width) for h in range(2)
    ]
    kept_parts = halves(kept)
    up_parts = halves(upstream)
    stored = jnp.concatenate(kept_parts, axis=0)
    back_away = (project(stored, weight, nbr) * Z_SCALE).astype(jnp.float16)
    rows = recv * cut
    back_got = [swap_tensor(back_away[:rows]), swap_tensor(back_away[rows:])]
    forward_own = project(inputs, weight, own)
    back_own = project(stored, weight, own)
    turned = stored.T.reshape(chips, 2, width // replicas, 2 * rows)
    mine = lax.dynamic_index_in_dim(turned, core, 1, keepdims=False).reshape(width // 2, 2 * rows)
    other = lax.dynamic_index_in_dim(turned, 1 - core, 1, keepdims=False)
    other = other.reshape(width // 2, 2 * rows)

    forward_z = forward_own + forward_away.astype(jnp.float32) * Z_BACK
    live = (slot < counts[0, 0]).astype(jnp.float32)
    live_rows = jnp.broadcast_to(live[:, None], (slots, tokens)).reshape(slots * tokens, 1)
    outputs = ((inputs.astype(jnp.float32) + jax.nn.silu(forward_z)) * live_rows).astype(
        jnp.bfloat16
    )
    outputs = shift(outputs.reshape(slots, tokens, width), "section", 1)
    packed = pick(source, outputs).reshape(replicas, cap, tokens, width)
    arrived = lax.all_to_all(packed, "replica", split_axis=0, concat_axis=0, tiled=True)

    gates, gates_nbr, returned = [], [], []
    for h in range(2):
        z = back_own[h * rows : (h + 1) * rows] + back_got[h].astype(jnp.float32) * Z_BACK
        g = jax.nn.sigmoid(z)
        slope = g * (1.0 + z * (1.0 - g))
        gate = (up_parts[h].astype(jnp.float32) * slope * mask).astype(jnp.bfloat16)
        gates.append(gate)
        gates_nbr.append(swap_tensor(gate))
    for h in range(2):
        grad = back_project(gates[h], gates_nbr[h], weight, own, up_parts[h], mask)
        grad = grad.reshape(replicas, cap, cut, width)
        back = lax.all_to_all(grad, "replica", split_axis=0, concat_axis=0, tiled=True)
        chosen = pick(place, back.reshape(recv, cut, width))
        returned.append(shift(chosen, "section", -1))
    returned = jnp.concatenate(returned, axis=1)

    block = (chips, width // replicas, width)
    send, keep = outer_sum(other, mine, gates[0], gates[1])
    sum_own = ring_sum(keep.reshape(block), send.reshape(block), scale_own)
    send, keep = outer_sum(other, mine, gates_nbr[0], gates_nbr[1])
    sum_nbr = ring_sum(keep.reshape(block), send.reshape(block), scale_nbr)
    first = own[0] == 0
    weight_grad = jnp.concatenate(
        [jnp.where(first, sum_own, sum_nbr), jnp.where(first, sum_nbr, sum_own)], axis=1
    )
    return (
        arrived.reshape(1, 1, recv, tokens, width),
        returned[None, None],
        weight_grad[None],
    )


def solution(mesh):
    placed = (
        P("section", "replica", None, None, "tensor"),
        P("section", "replica"),
        P("section", "replica", None, None),
        P("section", "tensor", None),
        P("section", "replica", None, None, "tensor"),
        P("section", "replica", None, None, "tensor"),
    )
    return jax.shard_map(
        local,
        mesh=mesh,
        in_specs=placed,
        out_specs=(
            P("section", "replica", None, None, "tensor"),
            P("section", "replica", None, None, "tensor"),
            P("section", ("tensor", "replica"), None),
        ),
        check_vma=False,
    )
```

time: 336 us -> 253 us (0.75)
  waiting for transfers between devices: 208 us -> 76.9 us
  starting transfers between devices: 28.1 us -> 73.5 us
  matrix products: 32.7 us -> 0 us
  Pallas kernels: 0 us -> 31.3 us
  other arithmetic: 5.9 us -> 32.1 us
  blocking collectives: 15.9 us -> 0 us
  between operations: 14.6 us -> 4.26 us
  local copies, waits for them, and re-layouts: 29.2 us -> 33.2 us
    reduce_scatter x2 -> x0, waiting for transfers between devices: 71.5 us -> none  [the longest x1 48.4 us: local(): lax.psum_scatter(backward_part, 'tensor', scatter_dimension=1, tiled=True)]
    ppermute x3 -> x26, waiting for transfers between devices: 28.5 us -> 76.7 us  [the longest x14 39 us: round_chips(): lax.ppermute(block, 'replica', [(r, (r + 2 * distance) % size) for r in r...]
    all_gather x1 -> x0, waiting for transfers between devices: 38.9 us -> none  [local(): gate_full = lax.all_gather(gate_grad, 'tensor', axis=1, tiled=True)]
    all_to_all x1 -> x3, waiting for transfers between devices: 34.2 us -> 0.2 us  [the longest x1 0.19 us: local(): lax.all_to_all(jnp.concatenate([flags, tops], axis=1), 'replica', split_a...]
    dot_general x7 -> x0, matrix products: 32.7 us -> none  [the longest x1 9.1 us: local(): lax.dot_general(stored, gate_full, (((0,), (0,)), ((), ())), preferred_el...]
    pallas_call x0 -> x11, Pallas kernels: none -> 31.3 us  [the longest x4 10 us: project(): pl.pallas_call(project_body, grid_spec=pltpu.PrefetchScalarGridSpec(num_s...]
    all_to_all x1, waiting for transfers between devices: 27.8 us -> 0.01 us  [local(): lax.all_to_all(packed, 'replica', split_axis=0, concat_axis=0, tiled=True)]
    ppermute x3 -> x26, starting transfers between devices: 14.4 us -> 41.7 us  [the longest x14 20 us: round_chips(): lax.ppermute(block, 'replica', [(r, (r + 2 * distance) % size) for r in r...]
  transfers between devices with their start and end apart: 9 -> 30, of which waited for: 8 -> 16; matrix products, arithmetic and copies ran while one was open for 15% -> 14% of each run, Pallas kernels for 0% -> 12%
where the time goes in v1:
time: 253 us; the launch traced here: 251 us
  waiting for transfers between devices  76.9 us (30%)
  starting transfers between devices  73.5 us (29%)
  local copies, waits for them, and re-layouts  33.2 us (13%)
  other arithmetic  32.1 us (13%)
  Pallas kernels  31.3 us (12%)
  between operations  4.26 us (2%)
    ppermute x14, waiting for transfers between devices, round_chips(): lax.ppermute(block, 'replica', [(r, (r + 2 * distance) % size) for r in r...  39 us
    ppermute x6, waiting for transfers between devices, swap_tensor(): return lax.ppermute(block, 'tensor', [(0, 1), (1, 0)])  37.4 us
    unnamed x39, local copies, waits for them, and re-layouts  24.5 us
    ppermute x14, starting transfers between devices, round_chips(): lax.ppermute(block, 'replica', [(r, (r + 2 * distance) % size) for r in r...  20 us
    ppermute x4, starting transfers between devices, shift(): return lax.ppermute(block, axis, route)  16.8 us
    all_to_all x2, starting transfers between devices, local(): lax.all_to_all(grad, 'replica', split_axis=0, concat_axis=0, tiled=True)  16 us
    convert_element_type x8, other arithmetic, ring_sum(): down = round_chips(s.astype(jnp.float16), -1)  10.5 us
    pallas_call x4, Pallas kernels, project(): pl.pallas_call(project_body, grid_spec=pltpu.PrefetchScalarGridSpec(num_s...  10 us
  transfers between devices with their start and end apart: 30, of which 16 were waited for; matrix products, arithmetic and copies ran while one was open for 14% of the time, Pallas kernels for 12%

profile of v1, /device:TPU:2, one launch (start us, length us, event | category | flops | bytes accessed | tf_op | source)
XLA Modules:
  0.0 251.3 jit_solution(3507096177844309653)
XLA Ops:
  2.0 5.1 %collective-permute-start = (s32[1,17]{1,0:T(1,128)S(1)}, s32[1,17]{1,0:T(1,128)S(1)}, u32[]{:S(2)}, u32[]{:S(2)}) collective-permute-start(s32[1,17]{1,0:T(1,128)S(1)} %add_bitcast_fusion), channel_id=1, source_target_pairs={{0,32},{32,64},{64,96},{96,128},{128,160},{160,192},{192,224},{1,3... | collective-permute-start | bytes 212 | tf_op jit(solution)/shard_map/ppermute | solution.py:17
  10.8 3.0 %shard_map.89 = f32[512,1280]{1,0:T(8,128)S(1)} custom-call(s32[1]{0:T(128)S(6)} %sub.22.half_ref, bf16[512,1280]{1,0:T(8,128)(2,1)S(1)} %get-tuple-element.29.x_ref, bf16[1280,2560]{1,0:T(8,128)(2,1)S(1)} %bitcast.125), custom_call_target="tpu_custom_call" | custom-call | flops 1677721600 | bytes 5898240 | tf_op jit(solution)/shard_map/pallas_call | solution.py:49
  22.4 8.6 %all-to-all-start.1 = ((bf16[16,1,4]{2,1,0:T(2,128)(2,1)}), bf16[16,1,4]{2,1,0:T(2,128)(2,1)S(1)}, u32[]{:S(2)}, u32[]{:S(2)}) async-start(bf16[16,1,4]{2,1,0:T(2,128)(2,1)} %copy.33), calls=%async_computation.1 | async-start | bytes 16384 | tf_op jit(solution)/shard_map/all_to_all | solution.py:199
  33.9 3.0 %shard_map.88 = f32[512,1280]{1,0:T(8,128)S(1)} custom-call(s32[1]{0:T(128)} %bitcast.8.half_ref, bf16[512,1280]{1,0:T(8,128)(2,1)S(1)} %get-tuple-element.29.x_ref, bf16[1280,2560]{1,0:T(8,128)(2,1)S(1)} %bitcast.126), custom_call_target="tpu_custom_call" | custom-call | flops 1677721600 | bytes 5898240 | tf_op jit(solution)/shard_map/pallas_call | solution.py:49
  39.0 6.7 %collective-permute-done.6 = f16[256,1280]{1,0:T(8,128)(2,1)} collective-permute-done((f16[256,1280]{1,0:T(8,128)(2,1)S(1)}, f16[256,1280]{1,0:T(8,128)(2,1)}, u32[]{:S(2)}, u32[]{:S(2)}) %collective-permute-start.6) | collective-permute-done | bytes 655392 | tf_op jit(solution)/shard_map/ppermute | solution.py:21
  45.7 3.3 %multiply_convert_fusion.2 = (bf16[256,1280]{1,0:T(8,128)(2,1)S(1)}, bf16[256,1280]{1,0:T(8,128)(2,1)S(1)}) fusion(f32[512,1280]{1,0:T(8,128)} %copy-done.6, f16[256,1280]{1,0:T(8,128)(2,1)} %collective-permute-done.3, f32[256]{0:T(256)S(1)} %mul.222, bf16[1,1,32,16,1280]{4,3,2,1,0:T(8,128)(2,1)S(1)} %copy-done.16, f16[256,1280]{1,0:T(8,128)(2,1)} %collective-permute-done.6), kind=kLoop, calls=%fused_computation.5 | loop fusion | flops 9175040 | bytes 6554624 | tf_op jit(solution)/shard_map/convert_element_type | solution.py:244
  55.0 4.3 %shard_map.94 = (f32[640,1280]{1,0:T(8,128)}, f32[640,1280]{1,0:T(8,128)S(1)}) custom-call(bf16[640,512]{1,0:T(8,128)(2,1)S(1)} %bitcast.150, bf16[640,512]{1,0:T(8,128)(2,1)S(1)} %bitcast.148, bf16[256,1280]{1,0:T(8,128)(2,1)S(1)} %get-tuple-element.24.own_ref.ga_ref, bf16[256,1280]{1,0:T(8,128)(2,1)S(1)} %get-tuple-element.25.own_ref.gb_ref), custom_call_target="tpu_custom_call" | custom-call | flops 1677721600 | bytes 6553600 | tf_op jit(solution)/shard_map/pallas_call | solution.py:110
  60.9 5.9 %collective-permute-done.4.nbr_ref.ga_ref = bf16[256,1280]{1,0:T(8,128)(2,1)S(1)} collective-permute-done((bf16[256,1280]{1,0:T(8,128)(2,1)S(1)}, bf16[256,1280]{1,0:T(8,128)(2,1)S(1)}, u32[]{:S(2)}, u32[]{:S(2)}) %collective-permute-start.4) | collective-permute-done | bytes 655392 | tf_op jit(solution)/shard_map/ppermute | solution.py:21
  66.8 11.7 %collective-permute-done.7.nbr_ref.gb_ref = bf16[256,1280]{1,0:T(8,128)(2,1)S(1)} collective-permute-done((bf16[256,1280]{1,0:T(8,128)(2,1)S(1)}, bf16[256,1280]{1,0:T(8,128)(2,1)S(1)}, u32[]{:S(2)}, u32[]{:S(2)}) %collective-permute-start.7) | collective-permute-done | bytes 655392 | tf_op jit(solution)/shard_map/ppermute | solution.py:21
  78.4 4.3 %shard_map.95 = (f32[640,1280]{1,0:T(8,128)}, f32[640,1280]{1,0:T(8,128)S(1)}) custom-call(bf16[640,512]{1,0:T(8,128)(2,1)S(1)} %bitcast.151, bf16[640,512]{1,0:T(8,128)(2,1)S(1)} %bitcast.149, bf16[256,1280]{1,0:T(8,128)(2,1)S(1)} %collective-permute-done.4.nbr_ref.ga_ref, bf16[256,1280]{1,0:T(8,128)(2,1)S(1)} %collective-permute-done.7.nbr_ref.gb_ref), custom_call_target="tpu_custom_call" | custom-call | flops 1677721600 | bytes 6553600 | tf_op jit(solution)/shard_map/pallas_call | solution.py:110
  87.5 4.0 %shard_map.90 = bf16[256,1280]{1,0:T(8,128)(2,1)} custom-call(s32[1]{0:T(128)} %bitcast.8.half_ref, bf16[256,1280]{1,0:T(8,128)(2,1)S(1)} %get-tuple-element.24.own_ref.ga_ref, bf16[256,1280]{1,0:T(8,128)(2,1)S(1)} %collective-permute-done.4.nbr_ref.ga_ref, bf16[1280,2560]{1,0:T(8,128)(2,1)S(1)} %bitcast.127, bf16[1280,2560]{1,0:T(8,128)(2,1)S(1)} %bitcast.128, ...), custom_call_target="tpu_custom_call" | custom-call | flops 1677721600 | bytes 7864320 | tf_op jit(solution)/shard_map/pallas_call | solution.py:76
  91.5 8.9 %all-to-all-start.2 = ((bf16[16,2,8,1280]{3,2,1,0:T(8,128)(2,1)}), bf16[16,2,8,1280]{3,2,1,0:T(8,128)(2,1)}, u32[]{:S(2)}, u32[]{:S(2)}) async-start(bf16[16,2,8,1280]{3,2,1,0:T(8,128)(2,1)} %bitcast.21), calls=%async_computation.2 | async-start | bytes 1310720 | tf_op jit(solution)/shard_map/all_to_all | solution.py:250
  107.1 2.9 %copy-done.4 = bf16[1,1280,2560]{2,1,0:T(8,128)(2,1)S(1)} copy-done((bf16[1,1280,2560]{2,1,0:T(8,128)(2,1)S(1)}, bf16[1,1280,2560]{2,1,0:T(8,128)(2,1)}, u32[]{:S(2)}) %copy-start.4) | copy-done | bytes 6553624
  115.0 4.0 %shard_map.92 = bf16[256,1280]{1,0:T(8,128)(2,1)} custom-call(s32[1]{0:T(128)} %bitcast.8.half_ref, bf16[256,1280]{1,0:T(8,128)(2,1)S(1)} %get-tuple-element.25.own_ref.gb_ref, bf16[256,1280]{1,0:T(8,128)(2,1)S(1)} %copy-done.15, bf16[1280,2560]{1,0:T(8,128)(2,1)S(1)} %bitcast.131, bf16[1280,2560]{1,0:T(8,128)(2,1)S(1)} %bitcast.132, ...), custom_call_target="tpu_custom_call" | custom-call | flops 1677721600 | bytes 7864320 | tf_op jit(solution)/shard_map/pallas_call | solution.py:76
  119.0 7.2 %all-to-all-start.3 = ((bf16[16,2,8,1280]{3,2,1,0:T(8,128)(2,1)}), bf16[16,2,8,1280]{3,2,1,0:T(8,128)(2,1)S(1)}, u32[]{:S(2)}, u32[]{:S(2)}) async-start(bf16[16,2,8,1280]{3,2,1,0:T(8,128)(2,1)} %bitcast.24), calls=%async_computation.3 | async-start | bytes 1310720 | tf_op jit(solution)/shard_map/all_to_all | solution.py:250
  128.6 4.7 %collective-permute-start.2 = (bf16[16,16,1280]{2,1,0:T(8,128)(2,1)}, bf16[16,16,1280]{2,1,0:T(8,128)(2,1)S(1)}, u32[]{:S(2)}, u32[]{:S(2)}) collective-permute-start(bf16[16,16,1280]{2,1,0:T(8,128)(2,1)} %bitcast.11), channel_id=1, source_target_pairs={{0,32},{32,64},{64,96},{96,128},{128,160},{160,192},{192,224},{1,3... | collective-permute-start | bytes 1966088 | tf_op jit(solution)/shard_map/ppermute | solution.py:17
  135.4 13.2 %collective-permute-done.18 = f32[1]{0:T(128)} collective-permute-done((f32[1]{0:T(128)}, f32[1]{0:T(128)}, u32[]{:S(2)}, u32[]{:S(2)}) %collective-permute-start.18) | collective-permute-done | bytes 36 | tf_op jit(solution)/shard_map/ppermute | solution.py:21
  154.1 3.7 %collective-permute-start.5 = (bf16[16,8,1280]{2,1,0:T(8,128)(2,1)}, bf16[16,8,1280]{2,1,0:T(8,128)(2,1)}, u32[]{:S(2)}, u32[]{:S(2)}) collective-permute-start(bf16[16,8,1280]{2,1,0:T(8,128)(2,1)} %shard_map.91), channel_id=1, source_target_pairs={{32,0},{64,32},{96,64},{128,96},{160,128},{192,160},{224,192},{33,... | collective-permute-start | bytes 983048 | tf_op jit(solution)/shard_map/ppermute | solution.py:17
  158.7 7.2 %all-to-all-start = ((bf16[16,2,16,1280]{3,2,1,0:T(8,128)(2,1)}), bf16[16,2,16,1280]{3,2,1,0:T(8,128)(2,1)}, u32[]{:S(2)}, u32[]{:S(2)}) async-start(bf16[16,2,16,1280]{3,2,1,0:T(8,128)(2,1)} %bitcast.12), calls=%async_computation | async-start | bytes 2621440 | tf_op jit(solution)/shard_map/all_to_all | solution.py:237
  167.7 3.3 %collective-permute-start.8 = (bf16[16,8,1280]{2,1,0:T(8,128)(2,1)S(1)}, bf16[16,8,1280]{2,1,0:T(8,128)(2,1)S(1)}, u32[]{:S(2)}, u32[]{:S(2)}) collective-permute-start(bf16[16,8,1280]{2,1,0:T(8,128)(2,1)S(1)} %shard_map.93), channel_id=1, source_target_pairs={{32,0},{64,32},{96,64},{128,96},{160,128},{192,160},{224,192},{33,... | collective-permute-start | bytes 983048 | tf_op jit(solution)/shard_map/ppermute | solution.py:17
  172.3 3.2 %collective-permute-start.10 = (f16[80,1280]{1,0:T(8,128)(2,1)S(1)}, f16[80,1280]{1,0:T(8,128)(2,1)S(1)}, u32[]{:S(2)}, u32[]{:S(2)}) collective-permute-start(f16[80,1280]{1,0:T(8,128)(2,1)S(1)} %get-tuple-element.22), channel_id=1, source_target_pairs={{0,28},{2,30},{4,0},{6,2},{8,4},{10,6},{12,8},{14,10},{16,12},{18,... | collective-permute-start | bytes 614408 | tf_op jit(solution)/shard_map/ppermute | solution.py:30
  177.1 3.3 %collective-permute-start.19 = (f16[80,1280]{1,0:T(8,128)(2,1)S(1)}, f16[80,1280]{1,0:T(8,128)(2,1)S(1)}, u32[]{:S(2)}, u32[]{:S(2)}) collective-permute-start(f16[80,1280]{1,0:T(8,128)(2,1)S(1)} %get-tuple-element.18), channel_id=1, source_target_pairs={{0,28},{2,30},{4,0},{6,2},{8,4},{10,6},{12,8},{14,10},{16,12},{18,... | collective-permute-start | bytes 614408 | tf_op jit(solution)/shard_map/ppermute | solution.py:30
  180.4 21.7 %collective-permute-done.10 = f16[80,1280]{1,0:T(8,128)(2,1)S(1)} collective-permute-done((f16[80,1280]{1,0:T(8,128)(2,1)S(1)}, f16[80,1280]{1,0:T(8,128)(2,1)S(1)}, u32[]{:S(2)}, u32[]{:S(2)}) %collective-permute-start.10) | collective-permute-done | bytes 204832 | tf_op jit(solution)/shard_map/ppermute | solution.py:30
  242.8 3.2 %collective-permute-done.25 = f16[80,1280]{1,0:T(8,128)(2,1)} collective-permute-done((f16[80,1280]{1,0:T(8,128)(2,1)}, f16[80,1280]{1,0:T(8,128)(2,1)}, u32[]{:S(2)}, u32[]{:S(2)}) %collective-permute-start.25) | collective-permute-done | bytes 204832 | tf_op jit(solution)/shard_map/ppermute | solution.py:30
  (141 shorter events, 101.0 us)
Async XLA Ops:
  2.0 17.9 %collective-permute-start = (s32[1,17]{1,0:T(1,128)S(1)}, s32[1,17]{1,0:T(1,128)S(1)}, u32[]{:S(2)}, u32[]{:S(2)}) collective-permute-start(s32[1,17]{1,0:T(1,128)S(1)} %add_bitcast_fusion), channel_id=1, source_target_pairs={{0,32},{32,64},{64,96},{96,128},{128,160},{160,192},{192,224},{1,3... | collective-permute-start | bytes 212 | tf_op jit(solution)/shard_map/ppermute | solution.py:17
  15.1 23.9 %collective-permute-start.3 = (f16[256,1280]{1,0:T(8,128)(2,1)}, f16[256,1280]{1,0:T(8,128)(2,1)}, u32[]{:S(2)}, u32[]{:S(2)}) collective-permute-start(f16[256,1280]{1,0:T(8,128)(2,1)} %get-tuple-element.32), channel_id=1, source_target_pairs={{0,1},{1,0},{2,3},{3,2},{4,5},{5,4},{6,7},{7,6},{8,9},{9,8},{10,11... | collective-permute-start | bytes 1966088 | tf_op jit(solution)/shard_map/ppermute | solution.py:21
  15.8 29.9 %collective-permute-start.6 = (f16[256,1280]{1,0:T(8,128)(2,1)S(1)}, f16[256,1280]{1,0:T(8,128)(2,1)}, u32[]{:S(2)}, u32[]{:S(2)}) collective-permute-start(f16[256,1280]{1,0:T(8,128)(2,1)S(1)} %get-tuple-element.33), channel_id=1, source_target_pairs={{0,1},{1,0},{2,3},{3,2},{4,5},{5,4},{6,7},{7,6},{8,9},{9,8},{10,11... | collective-permute-start | bytes 1966088 | tf_op jit(solution)/shard_map/ppermute | solution.py:21
  22.4 16.1 %all-to-all-start.1 = ((bf16[16,1,4]{2,1,0:T(2,128)(2,1)}), bf16[16,1,4]{2,1,0:T(2,128)(2,1)S(1)}, u32[]{:S(2)}, u32[]{:S(2)}) async-start(bf16[16,1,4]{2,1,0:T(2,128)(2,1)} %copy.33), calls=%async_computation.1 | async-start | bytes 16384 | tf_op jit(solution)/shard_map/all_to_all | solution.py:199
  49.0 17.8 %collective-permute-start.4 = (bf16[256,1280]{1,0:T(8,128)(2,1)S(1)}, bf16[256,1280]{1,0:T(8,128)(2,1)S(1)}, u32[]{:S(2)}, u32[]{:S(2)}) collective-permute-start(bf16[256,1280]{1,0:T(8,128)(2,1)S(1)} %get-tuple-element.24.own_ref.ga_ref), channel_id=1, source_target_pairs={{0,1},{1,0},{2,3},{3,2},{4,5},{5,4},{6,7},{7,6},{8,9},{9,8},{10,11... | collective-permute-start | bytes 1966088 | tf_op jit(solution)/shard_map/ppermute | solution.py:21
  49.8 28.6 %collective-permute-start.7 = (bf16[256,1280]{1,0:T(8,128)(2,1)S(1)}, bf16[256,1280]{1,0:T(8,128)(2,1)S(1)}, u32[]{:S(2)}, u32[]{:S(2)}) collective-permute-start(bf16[256,1280]{1,0:T(8,128)(2,1)S(1)} %get-tuple-element.25.own_ref.gb_ref), channel_id=1, source_target_pairs={{0,1},{1,0},{2,3},{3,2},{4,5},{5,4},{6,7},{7,6},{8,9},{9,8},{10,11... | collective-permute-start | bytes 1966088 | tf_op jit(solution)/shard_map/ppermute | solution.py:21
  60.9 110.1 %collective-permute-start.9 = (f32[8,80,1280]{2,1,0:T(8,128)}, f32[8,80,1280]{2,1,0:T(8,128)}, u32[]{:S(2)}, u32[]{:S(2)}) collective-permute-start(f32[8,80,1280]{2,1,0:T(8,128)} %bitcast.32), channel_id=1, source_target_pairs={{0,2},{2,0},{4,6},{6,4},{8,10},{10,8},{12,14},{14,12},{16,18},{18,... | collective-permute-start | bytes 9830408 | tf_op jit(solution)/shard_map/ppermute | solution.py:25
  84.5 91.0 %collective-permute-start.17 = (f32[8,80,1280]{2,1,0:T(8,128)}, f32[8,80,1280]{2,1,0:T(8,128)}, u32[]{:S(2)}, u32[]{:S(2)}) collective-permute-start(f32[8,80,1280]{2,1,0:T(8,128)} %bitcast.43), channel_id=1, source_target_pairs={{0,2},{2,0},{4,6},{6,4},{8,10},{10,8},{12,14},{14,12},{16,18},{18,... | collective-permute-start | bytes 9830408 | tf_op jit(solution)/shard_map/ppermute | solution.py:25
  91.5 27.4 %all-to-all-start.2 = ((bf16[16,2,8,1280]{3,2,1,0:T(8,128)(2,1)}), bf16[16,2,8,1280]{3,2,1,0:T(8,128)(2,1)}, u32[]{:S(2)}, u32[]{:S(2)}) async-start(bf16[16,2,8,1280]{3,2,1,0:T(8,128)(2,1)} %bitcast.21), calls=%async_computation.2 | async-start | bytes 1310720 | tf_op jit(solution)/shard_map/all_to_all | solution.py:250
  106.3 19.8 %collective-permute-start.1 = (f16[256,1280]{1,0:T(8,128)(2,1)}, f16[256,1280]{1,0:T(8,128)(2,1)}, u32[]{:S(2)}, u32[]{:S(2)}) collective-permute-start(f16[256,1280]{1,0:T(8,128)(2,1)} %multiply_convert_fusion.4), channel_id=1, source_target_pairs={{0,1},{1,0},{2,3},{3,2},{4,5},{5,4},{6,7},{7,6},{8,9},{9,8},{10,11... | collective-permute-start | bytes 1966088 | tf_op jit(solution)/shard_map/ppermute | solution.py:21
  119.0 38.9 %all-to-all-start.3 = ((bf16[16,2,8,1280]{3,2,1,0:T(8,128)(2,1)}), bf16[16,2,8,1280]{3,2,1,0:T(8,128)(2,1)S(1)}, u32[]{:S(2)}, u32[]{:S(2)}) async-start(bf16[16,2,8,1280]{3,2,1,0:T(8,128)(2,1)} %bitcast.24), calls=%async_computation.3 | async-start | bytes 1310720 | tf_op jit(solution)/shard_map/all_to_all | solution.py:250
  128.6 21.6 %collective-permute-start.2 = (bf16[16,16,1280]{2,1,0:T(8,128)(2,1)}, bf16[16,16,1280]{2,1,0:T(8,128)(2,1)S(1)}, u32[]{:S(2)}, u32[]{:S(2)}) collective-permute-start(bf16[16,16,1280]{2,1,0:T(8,128)(2,1)} %bitcast.11), channel_id=1, source_target_pairs={{0,32},{32,64},{64,96},{96,128},{128,160},{160,192},{192,224},{1,3... | collective-permute-start | bytes 1966088 | tf_op jit(solution)/shard_map/ppermute | solution.py:17
  135.3 13.3 %collective-permute-start.18 = (f32[1]{0:T(128)}, f32[1]{0:T(128)}, u32[]{:S(2)}, u32[]{:S(2)}) collective-permute-start(f32[1]{0:T(128)} %bitcast.44), channel_id=1, source_target_pairs={{0,1},{1,0},{2,3},{3,2},{4,5},{5,4},{6,7},{7,6},{8,9},{9,8},{10,11... | collective-permute-start | bytes 20 | tf_op jit(solution)/shard_map/ppermute | solution.py:21
  154.1 84.6 %collective-permute-start.5 = (bf16[16,8,1280]{2,1,0:T(8,128)(2,1)}, bf16[16,8,1280]{2,1,0:T(8,128)(2,1)}, u32[]{:S(2)}, u32[]{:S(2)}) collective-permute-start(bf16[16,8,1280]{2,1,0:T(8,128)(2,1)} %shard_map.91), channel_id=1, source_target_pairs={{32,0},{64,32},{96,64},{128,96},{160,128},{192,160},{224,192},{33,... | collective-permute-start | bytes 983048 | tf_op jit(solution)/shard_map/ppermute | solution.py:17
  158.7 83.7 %all-to-all-start = ((bf16[16,2,16,1280]{3,2,1,0:T(8,128)(2,1)}), bf16[16,2,16,1280]{3,2,1,0:T(8,128)(2,1)}, u32[]{:S(2)}, u32[]{:S(2)}) async-start(bf16[16,2,16,1280]{3,2,1,0:T(8,128)(2,1)} %bitcast.12), calls=%async_computation | async-start | bytes 2621440 | tf_op jit(solution)/shard_map/all_to_all | solution.py:237
  167.7 72.8 %collective-permute-start.8 = (bf16[16,8,1280]{2,1,0:T(8,128)(2,1)S(1)}, bf16[16,8,1280]{2,1,0:T(8,128)(2,1)S(1)}, u32[]{:S(2)}, u32[]{:S(2)}) collective-permute-start(bf16[16,8,1280]{2,1,0:T(8,128)(2,1)S(1)} %shard_map.93), channel_id=1, source_target_pairs={{32,0},{64,32},{96,64},{128,96},{160,128},{192,160},{224,192},{33,... | collective-permute-start | bytes 983048 | tf_op jit(solution)/shard_map/ppermute | solution.py:17
  172.3 29.8 %collective-permute-start.10 = (f16[80,1280]{1,0:T(8,128)(2,1)S(1)}, f16[80,1280]{1,0:T(8,128)(2,1)S(1)}, u32[]{:S(2)}, u32[]{:S(2)}) collective-permute-start(f16[80,1280]{1,0:T(8,128)(2,1)S(1)} %get-tuple-element.22), channel_id=1, source_target_pairs={{0,28},{2,30},{4,0},{6,2},{8,4},{10,6},{12,8},{14,10},{16,12},{18,... | collective-permute-start | bytes 614408 | tf_op jit(solution)/shard_map/ppermute | solution.py:30
  175.4 42.8 %collective-permute-start.14 = (f16[80,1280]{1,0:T(8,128)(2,1)S(1)}, f16[80,1280]{1,0:T(8,128)(2,1)S(1)}, u32[]{:S(2)}, u32[]{:S(2)}) collective-permute-start(f16[80,1280]{1,0:T(8,128)(2,1)S(1)} %get-tuple-element.23), channel_id=1, source_target_pairs={{0,4},{2,6},{4,8},{6,10},{8,12},{10,14},{12,16},{14,18},{16,20},{1... | collective-permute-start | bytes 614408 | tf_op jit(solution)/shard_map/ppermute | solution.py:30
  177.1 29.4 %collective-permute-start.19 = (f16[80,1280]{1,0:T(8,128)(2,1)S(1)}, f16[80,1280]{1,0:T(8,128)(2,1)S(1)}, u32[]{:S(2)}, u32[]{:S(2)}) collective-permute-start(f16[80,1280]{1,0:T(8,128)(2,1)S(1)} %get-tuple-element.18), channel_id=1, source_target_pairs={{0,28},{2,30},{4,0},{6,2},{8,4},{10,6},{12,8},{14,10},{16,12},{18,... | collective-permute-start | bytes 614408 | tf_op jit(solution)/shard_map/ppermute | solution.py:30
  207.5 8.1 %collective-permute-start.20 = (f16[80,1280]{1,0:T(8,128)(2,1)S(1)}, f16[80,1280]{1,0:T(8,128)(2,1)S(1)}, u32[]{:S(2)}, u32[]{:S(2)}) collective-permute-start(f16[80,1280]{1,0:T(8,128)(2,1)S(1)} %fusion.2), channel_id=1, source_target_pairs={{0,28},{2,30},{4,0},{6,2},{8,4},{10,6},{12,8},{14,10},{16,12},{18,... | collective-permute-start | bytes 614408 | tf_op jit(solution)/shard_map/ppermute | solution.py:30
  221.4 21.0 %collective-permute-start.13 = (f16[80,1280]{1,0:T(8,128)(2,1)S(1)}, f16[80,1280]{1,0:T(8,128)(2,1)}, u32[]{:S(2)}, u32[]{:S(2)}) collective-permute-start(f16[80,1280]{1,0:T(8,128)(2,1)S(1)} %get-tuple-element.20), channel_id=1, source_target_pairs={{0,28},{2,30},{4,0},{6,2},{8,4},{10,6},{12,8},{14,10},{16,12},{18,... | collective-permute-start | bytes 614408 | tf_op jit(solution)/shard_map/ppermute | solution.py:30
  222.6 9.1 %collective-permute-start.15 = (f16[80,1280]{1,0:T(8,128)(2,1)S(1)}, f16[80,1280]{1,0:T(8,128)(2,1)S(1)}, u32[]{:S(2)}, u32[]{:S(2)}) collective-permute-start(f16[80,1280]{1,0:T(8,128)(2,1)S(1)} %get-tuple-element.21), channel_id=1, source_target_pairs={{0,4},{2,6},{4,8},{6,10},{8,12},{10,14},{12,16},{14,18},{16,20},{1... | collective-permute-start | bytes 614408 | tf_op jit(solution)/shard_map/ppermute | solution.py:30
  228.3 8.4 %collective-permute-start.24 = (f16[80,1280]{1,0:T(8,128)(2,1)S(1)}, f16[80,1280]{1,0:T(8,128)(2,1)S(1)}, u32[]{:S(2)}, u32[]{:S(2)}) collective-permute-start(f16[80,1280]{1,0:T(8,128)(2,1)S(1)} %get-tuple-element.17), channel_id=1, source_target_pairs={{0,4},{2,6},{4,8},{6,10},{8,12},{10,14},{12,16},{14,18},{16,20},{1... | collective-permute-start | bytes 614408 | tf_op jit(solution)/shard_map/ppermute | solution.py:30
  233.4 9.0 %collective-permute-start.16 = (f16[80,1280]{1,0:T(8,128)(2,1)}, f16[80,1280]{1,0:T(8,128)(2,1)}, u32[]{:S(2)}, u32[]{:S(2)}) collective-permute-start(f16[80,1280]{1,0:T(8,128)(2,1)} %fusion.8), channel_id=1, source_target_pairs={{0,4},{2,6},{4,8},{6,10},{8,12},{10,14},{12,16},{14,18},{16,20},{1... | collective-permute-start | bytes 614408 | tf_op jit(solution)/shard_map/ppermute | solution.py:30
  (25 other events, 157.1 us)

commit v2 on v0

v2 whole, which is shorter than its diff:
```python
import jax
import jax.numpy as jnp
from jax import lax
from jax.experimental import pallas as pl
from jax.experimental.pallas import tpu as pltpu
from jax.sharding import PartitionSpec as P

Z_SCALE = 64.0
Z_BACK = 1.0 / 64.0
TILE = 256
VMEM_BYTES = 24 * 1024 * 1024

def shift(block, axis, distance):
    devices = range(lax.axis_size(axis))
    route = [(i, i + distance) for i in devices if i + distance in devices]
    return lax.ppermute(block, axis, route)


def swap_tensor(block):
    return lax.ppermute(block, "tensor", [(0, 1), (1, 0)])


def swap_core(block):
    return lax.ppermute(block, "replica", [(r, r ^ 1) for r in range(lax.axis_size("replica"))])


def round_chips(block, distance):
    size = lax.axis_size("replica")
    return lax.ppermute(block, "replica", [(r, (r + 2 * distance) % size) for r in range(size)])


def shaped(shape, dtype):
    return jax.ShapeDtypeStruct(shape, dtype)


def in_hbm(x):
    return pltpu.with_memory_space_constraint(x, pltpu.HBM)


def kernel(body, out_shape, operands, spaces, scratch=(), out_space=pltpu.VMEM, aliases=None):
    single = not isinstance(out_shape, list)
    spec = pl.BlockSpec(memory_space=out_space)
    return pl.pallas_call(
        body,
        in_specs=[pl.BlockSpec(memory_space=space) for space in spaces],
        out_specs=spec if single else [spec] * len(out_shape),
        out_shape=out_shape,
        scratch_shapes=list(scratch),
        input_output_aliases=aliases or {},
        compiler_params=pltpu.CompilerParams(vmem_limit_bytes=VMEM_BYTES),
        cost_estimate=pl.CostEstimate(flops=1024, bytes_accessed=1024, transcendentals=0),
    )(*operands)


def project_body(half_ref, x_ref, w_ref, o_ref, held, sems, *out):
    tiles, _, tile = held.shape
    base = half_ref[0] * (tiles * tile)

    def fetch(j):
        at = pl.multiple_of(base + j * tile, tile)
        return pltpu.make_async_copy(w_ref.at[:, pl.ds(at, tile)], held.at[j], sems.at[j])

    for j in range(tiles):
        fetch(j).start()

    def step(j, carry):
        fetch(j).wait()
        z = jnp.dot(x_ref[...], held[j], preferred_element_type=jnp.float32)
        if out:
            out[0][j] = z
            store(j).start()
        else:
            o_ref[:, pl.ds(pl.multiple_of(j * tile, tile), tile)] = z
        return carry

    def store(j):
        at = pl.ds(pl.multiple_of(j * tile, tile), tile)
        return pltpu.make_async_copy(out[0].at[j], o_ref.at[:, at], out[1].at[j])

    lax.fori_loop(0, tiles, step, 0)
    if out:
        for j in range(tiles):
            store(j).wait()


def project(x, weight, half, keep=False):
    rows, depth = x.shape
    width = weight.shape[1] // 2
    tiles = width // TILE
    scratch = [pltpu.VMEM((tiles, depth, TILE), weight.dtype), pltpu.SemaphoreType.DMA((tiles,))]
    if keep:
        scratch += [pltpu.VMEM((tiles, rows, TILE), jnp.float32), pltpu.SemaphoreType.DMA((tiles,))]
    return kernel(
        project_body,
        pltpu.HBM((rows, width), jnp.float32) if keep else shaped((rows, width), jnp.float32),
        (half, x, in_hbm(weight)),
        (pltpu.SMEM, pltpu.VMEM, pl.ANY),
        scratch,
        pltpu.HBM if keep else pltpu.VMEM,
    )


def back_body(row, half_ref, own_ref, nbr_ref, w_ref, up_ref, mask_ref, *rest):
    o_ref, held, sems, grads, out_sems = rest[-5:]
    tiles, tile, _ = held.shape
    rows, depth = own_ref.shape
    own_at = pl.multiple_of(half_ref[0] * depth, tile)
    nbr_at = pl.multiple_of((1 - half_ref[0]) * depth, tile)
    dims = (((1,), (1,)), ((), ()))
    here = pl.ds(row, rows)

    def fetch(j):
        at = pl.multiple_of(j * tile, tile)
        return pltpu.make_async_copy(w_ref.at[pl.ds(at, tile)], held.at[j], sems.at[j])

    def store(j):
        at = pl.ds(pl.multiple_of(j * tile, tile), tile)
        return pltpu.make_async_copy(grads.at[j], o_ref.at[here, at], out_sems.at[j])

    for j in range(tiles):
        fetch(j).start()

    def step(j, carry):
        fetch(j).wait()
        at = pl.ds(pl.multiple_of(j * tile, tile), tile)
        terms = lax.dot_general(
            own_ref[...], held[j, :, pl.ds(own_at, depth)], dims, preferred_element_type=jnp.float32
        )
        terms += lax.dot_general(
            nbr_ref[...], held[j, :, pl.ds(nbr_at, depth)], dims, preferred_element_type=jnp.float32
        )
        up = up_ref[here, at].astype(jnp.float32)
        grads[j] = ((up + terms) * mask_ref[here, :]).astype(jnp.bfloat16)
        store(j).start()
        return carry

    lax.fori_loop(0, tiles, step, 0)
    for j in range(tiles):
        store(j).wait()


def back_project(own, nbr, weight, half, up, mask, row, before=None):
    width = weight.shape[0]
    tiles = width // TILE
    operands = (half, own, nbr, in_hbm(weight), up, mask)
    spaces = (pltpu.SMEM, pltpu.VMEM, pltpu.VMEM, pl.ANY, pltpu.VMEM, pltpu.VMEM)
    aliases = {}
    if before is not None:
        aliases = {len(operands): 0}
        operands, spaces = operands + (before,), spaces + (pl.ANY,)

    def body(*refs):
        back_body(row, *refs)

    return kernel(
        body,
        pltpu.HBM(up.shape, jnp.bfloat16),
        operands,
        spaces,
        [
            pltpu.VMEM((tiles, TILE, 2 * width), weight.dtype),
            pltpu.SemaphoreType.DMA((tiles,)),
            pltpu.VMEM((tiles, own.shape[0], TILE), jnp.bfloat16),
            pltpu.SemaphoreType.DMA((tiles,)),
        ],
        pltpu.HBM,
        aliases,
    )


def outer_body(other_ref, mine_ref, ga_ref, gb_ref, mask_ref, send_ref, keep_ref, sent, kept, sems):
    tiles, _, tile = kept.shape
    rows = ga_ref.shape[0]

    def store(j, i):
        at = pl.ds(pl.multiple_of(j * tile, tile), tile)
        out, ref = ((sent, send_ref), (kept, keep_ref))[i]
        return pltpu.make_async_copy(out.at[j], ref.at[:, at], sems.at[j, i])

    def step(j, carry):
        at = pl.ds(pl.multiple_of(j * tile, tile), tile)
        ga = (ga_ref[:, at].astype(jnp.float32) * mask_ref[:rows]).astype(jnp.bfloat16)
        gb = (gb_ref[:, at].astype(jnp.float32) * mask_ref[rows:]).astype(jnp.bfloat16)
        for i, lhs, out in ((0, other_ref, sent), (1, mine_ref, kept)):
            total = jnp.dot(lhs[:, :rows], ga, preferred_element_type=jnp.float32)
            total += jnp.dot(lhs[:, rows:], gb, preferred_element_type=jnp.float32)
            out[j] = total.astype(out.dtype)
            store(j, i).start()
        return carry

    lax.fori_loop(0, tiles, step, 0)
    for j in range(tiles):
        for i in range(2):
            store(j, i).wait()


def outer_sum(other, mine, gate_a, gate_b, mask):
    depth, width = other.shape[0], gate_a.shape[1]
    tiles = width // TILE
    return kernel(
        outer_body,
        [pltpu.HBM((depth, width), jnp.bfloat16), pltpu.HBM((depth, width), jnp.float32)],
        (other, mine, gate_a, gate_b, mask),
        (pltpu.VMEM,) * 5,
        [
            pltpu.VMEM((tiles, depth, TILE), jnp.bfloat16),
            pltpu.VMEM((tiles, depth, TILE), jnp.float32),
            pltpu.SemaphoreType.DMA((tiles, 2)),
        ],
        pltpu.HBM,
    )


def pick_body(index_ref, x_ref, o_ref):
    def step(i, carry):
        source = index_ref[i]
        block = x_ref[jnp.maximum(source, 0)]
        o_ref[i] = jnp.where(source >= 0, block, jnp.zeros_like(block))
        return carry

    lax.fori_loop(0, o_ref.shape[0], step, 0)


def pick(index, x):
    shape = shaped((index.shape[0],) + x.shape[1:], x.dtype)
    return kernel(pick_body, shape, (index, x), (pltpu.SMEM, pltpu.VMEM))


class Order:
    def __init__(self):
        self.last = None

    def tie(self, *arrays):
        if self.last is None:
            return arrays
        return lax.optimization_barrier(arrays + (self.last,))[:-1]

    def mark(self, array):
        self.last = array
        return array

    def here(self, *arrays):
        arrays = self.tie(*arrays)
        self.last = arrays[0]
        return arrays


class Ring:
    def __init__(self, order, keep, send):
        self.order, self.keep = order, keep
        self.got = swap_core(send)
        self.down = self.up = None
        self.next = lax.axis_size("replica") // 4

    def term(self, keep, got, offset, extra):
        chips = lax.axis_size("replica") // 2
        at = (lax.axis_index("replica") // 2 + offset + chips) % chips
        s = lax.dynamic_index_in_dim(keep, at, 0, keepdims=False)
        s = s + lax.dynamic_index_in_dim(got, at, 0, keepdims=False).astype(jnp.float32)
        return s if extra is None else s + extra.astype(jnp.float32)

    def round(self):
        k = self.next
        far = lax.axis_size("replica") // 4
        held = [self.keep, self.got] + [v for v in (self.down, self.up) if v is not None]
        held = list(self.order.tie(*held))
        self.keep, self.got = held[:2]
        cut = self.keep.shape[-1] // 2
        if k == far:
            sent = self.term(self.keep, self.got, k, None).astype(jnp.bfloat16)
            self.order.mark(sent)
            self.down = round_chips(sent[:, :cut], -1)
            self.up = round_chips(sent[:, cut:], 1)
        elif k == 0:
            total = self.term(self.keep, self.got, 0, held[2]) + held[3].astype(jnp.float32)
            return self.order.mark(total)
        else:
            down, up = held[2:]
            if k == far - 1:
                down = jnp.pad(down, ((0, 0), (0, cut)))
                up = jnp.pad(up, ((0, 0), (cut, 0)))
            sent = self.term(self.keep, self.got, -k, down).astype(jnp.bfloat16)
            self.down = round_chips(sent, -1)
            sent = self.term(self.keep, self.got, k, up).astype(jnp.bfloat16)
            self.up = round_chips(sent, 1)
            self.order.mark(sent)
        self.next = k - 1


def local(fresh, counts, wiring, weights, kept, upstream):
    replicas = lax.axis_size("replica")
    chips = replicas // 2
    slots, tokens, width = fresh.shape[2:]
    recv = kept.shape[2]
    cap = recv // replicas
    rows = recv * tokens // 2
    weight = weights[0]
    inputs = fresh[0, 0].reshape(slots * tokens, width)
    stored = kept[0, 0].reshape(2 * rows, width)
    up = upstream[0, 0].reshape(2 * rows, width)
    own = lax.axis_index("tensor").astype(jnp.int32)[None]
    nbr = 1 - own
    core = lax.axis_index("replica") % 2
    order = Order()

    back_nbr = order.mark(project(stored, weight, nbr))

    def send_half(h):
        (x,) = order.tie(back_nbr)
        sent = (x[h * rows : (h + 1) * rows] * Z_SCALE).astype(jnp.float16)
        return swap_tensor(order.mark(sent))

    back_got = [send_half(0)]
    (words,) = order.tie(jnp.concatenate([wiring[0, 0, :, 0], counts[0]])[None])
    plan = shift(order.mark(words), "section", 1)[0]
    back_got.append(send_half(1))

    (x,) = order.tie(stored)
    back_own = order.mark(project(x, weight, own, True))
    (x,) = order.tie(stored)
    turned = x.T.reshape(chips, 2, width // replicas, 2 * rows)
    mine = lax.dynamic_index_in_dim(turned, core, 1, keepdims=False).reshape(width // 2, 2 * rows)
    other = lax.dynamic_index_in_dim(turned, 1 - core, 1, keepdims=False)
    other = order.mark(other.reshape(width // 2, 2 * rows))

    def gate_half(h):
        here = slice(h * rows, (h + 1) * rows)
        z_own, z_got, u = order.tie(back_own, back_got[h], up)
        z = z_own[here] + z_got.astype(jnp.float32) * Z_BACK
        g = jax.nn.sigmoid(z)
        slope = g * (1.0 + z * (1.0 - g))
        return order.mark((u[here].astype(jnp.float32) * slope).astype(jnp.bfloat16))

    def back_half(h, before=None):
        gate, got, u = order.tie(gates[h], gates_nbr[h], up)
        return order.mark(back_project(gate, got, weight, own, u, mask, h * rows, before))

    def across(block):
        return lax.all_to_all(block, "replica", split_axis=0, concat_axis=0, tiled=True)

    def ring_of(first, second):
        first, second = order.tie(first, second)
        send, keep = outer_sum(other, mine, first, second, mask)
        order.mark(keep)
        shape = (chips, width // replicas, width)
        return Ring(order, keep.reshape(shape), send.reshape(shape))

    gates = [gate_half(0)]
    gates_nbr = [swap_tensor(gates[0])]

    (plan,) = order.tie(plan)
    target, count = plan[:slots], plan[slots]
    slot = jnp.arange(slots)
    same = target[:, None] == target[None, :]
    rank = jnp.sum(same & (slot[None, :] < slot[:, None]), axis=1).astype(jnp.int32)
    place = target * cap + rank
    hit = (place[None, :] == jnp.arange(recv)[:, None]) & (slot < count)[None, :]
    source = (jnp.sum(jnp.where(hit, slot[None, :] + 1, 0), axis=1) - 1).astype(jnp.int32)
    flags = order.mark((source >= 0).astype(jnp.bfloat16).reshape(replicas, cap))
    told = across(flags)
    gates.append(gate_half(1))
    gates_nbr.append(swap_tensor(gates[1]))
    (told,) = order.tie(told)
    marks = told.reshape(recv).astype(jnp.float32)
    mask = order.mark(jnp.broadcast_to(marks[:, None], (recv, tokens)).reshape(2 * rows, 1))

    (x,) = order.tie(inputs)
    sent = order.mark((project(x, weight, nbr) * Z_SCALE).astype(jnp.float16))
    forward_got = swap_tensor(sent)
    (x,) = order.tie(inputs)
    forward_own = order.mark(project(x, weight, own, True))

    grads = back_half(0)
    ring_own = ring_of(gates[0], gates[1])
    grads = back_half(1, grads)
    back = across(grads.reshape(replicas, cap, tokens, width))

    forward_own, forward_got, x = order.tie(forward_own, forward_got, inputs)
    forward_z = forward_own + forward_got.astype(jnp.float32) * Z_BACK
    live = (slot < counts[0, 0]).astype(jnp.float32)
    live_rows = jnp.broadcast_to(live[:, None], (slots, tokens)).reshape(slots * tokens, 1)
    outputs = ((x.astype(jnp.float32) + jax.nn.silu(forward_z)) * live_rows).astype(jnp.bfloat16)
    order.mark(outputs)
    outputs = shift(outputs.reshape(slots, tokens, width), "section", 1)

    ring_nbr = ring_of(gates_nbr[0], gates_nbr[1])
    ring_own.round()
    ring_nbr.round()
    (outputs,) = order.tie(outputs)
    packed = order.mark(pick(source, outputs))
    arrived = across(packed.reshape(replicas, cap, tokens, width))
    (back,) = order.tie(back)
    returned = order.mark(pick(place, back.reshape(recv, tokens, width)))
    returned = shift(returned, "section", -1)
    ring_own.round()
    ring_nbr.round()
    ring_own.round()
    ring_nbr.round()
    ring_own.round()
    ring_nbr.round()
    sum_own = ring_own.round()
    sum_nbr = ring_nbr.round()
    zero = jnp.zeros((), jnp.int32)
    weight_grad = jnp.zeros((width // replicas, 2 * width), jnp.float32)
    weight_grad = lax.dynamic_update_slice(weight_grad, sum_own, (zero, own[0] * width))
    weight_grad = lax.dynamic_update_slice(weight_grad, sum_nbr, (zero, nbr[0] * width))
    return (
        arrived.reshape(1, 1, recv, tokens, width),
        returned[None, None],
        weight_grad[None],
    )


def solution(mesh):
    placed = (
        P("section", "replica", None, None, "tensor"),
        P("section", "replica"),
        P("section", "replica", None, None),
        P("section", "tensor", None),
        P("section", "replica", None, None, "tensor"),
        P("section", "replica", None, None, "tensor"),
    )
    return jax.shard_map(
        local,
        mesh=mesh,
        in_specs=placed,
        out_specs=(
            P("section", "replica", None, None, "tensor"),
            P("section", "replica", None, None, "tensor"),
            P("section", ("tensor", "replica"), None),
        ),
        check_vma=False,
    )
```

time: 336 us -> 191 us (0.57)
  waiting for transfers between devices: 208 us -> 54.3 us
  Pallas kernels: 0 us -> 39.9 us
  starting transfers between devices: 28.1 us -> 61.5 us
  matrix products: 32.7 us -> 0 us
  local copies, waits for them, and re-layouts: 29.2 us -> 8.48 us
  other arithmetic: 5.9 us -> 24.2 us
  blocking collectives: 15.9 us -> 0 us
  between operations: 14.6 us -> 1.73 us
    reduce_scatter x2 -> x0, waiting for transfers between devices: 71.5 us -> none  [the longest x1 48.4 us: local(): lax.psum_scatter(backward_part, 'tensor', scatter_dimension=1, tiled=True)]
    all_to_all x2 -> x3, waiting for transfers between devices: 62 us -> 4.77 us  [across(): lax.all_to_all(block, 'replica', split_axis=0, concat_axis=0, tiled=True)]
    pallas_call x0 -> x10, Pallas kernels: none -> 39.9 us  [kernel(): pl.pallas_call(body, in_specs=[pl.BlockSpec(memory_space=space) for space...]
    all_gather x1 -> x0, waiting for transfers between devices: 38.9 us -> none  [local(): gate_full = lax.all_gather(gate_grad, 'tensor', axis=1, tiled=True)]
    dot_general x7 -> x0, matrix products: 32.7 us -> none  [the longest x1 9.1 us: local(): lax.dot_general(stored, gate_full, (((0,), (0,)), ((), ())), preferred_el...]
    ppermute x3 -> x26, starting transfers between devices: 14.4 us -> 39.9 us  [the longest x16 21 us: round_chips(): lax.ppermute(block, 'replica', [(r, (r + 2 * distance) % size) for r in r...]
    ppermute x3 -> x26, waiting for transfers between devices: 28.5 us -> 49.5 us  [the longest x16 37.5 us: round_chips(): lax.ppermute(block, 'replica', [(r, (r + 2 * distance) % size) for r in r...]
    all_to_all x1 -> x0, blocking collectives: 15.9 us -> none  [local(): lax.all_to_all(flags, 'replica', split_axis=0, concat_axis=0, tiled=True)]
  transfers between devices with their start and end apart: 9 -> 29, of which waited for: 8 -> 13; matrix products, arithmetic and copies ran while one was open for 15% -> 15% of each run, Pallas kernels for 0% -> 19%
where the time goes in v2:
time: 191 us; the launch traced here: 190 us
  starting transfers between devices  61.5 us (32%)
  waiting for transfers between devices  54.3 us (28%)
  Pallas kernels  39.9 us (21%)
  other arithmetic  24.2 us (13%)
  local copies, waits for them, and re-layouts  8.48 us (4%)
    pallas_call x10, Pallas kernels, kernel(): pl.pallas_call(body, in_specs=[pl.BlockSpec(memory_space=space) for space...  39.9 us
    ppermute x16, waiting for transfers between devices, round_chips(): lax.ppermute(block, 'replica', [(r, (r + 2 * distance) % size) for r in r...  37.5 us
    all_to_all x3, starting transfers between devices, across(): lax.all_to_all(block, 'replica', split_axis=0, concat_axis=0, tiled=True)  21.7 us
    ppermute x16, starting transfers between devices, round_chips(): lax.ppermute(block, 'replica', [(r, (r + 2 * distance) % size) for r in r...  21 us
    ppermute x3, starting transfers between devices, shift(): return lax.ppermute(block, axis, route)  14 us
    ppermute x3, waiting for transfers between devices, shift(): return lax.ppermute(block, axis, route)  8.59 us
    convert_element_type x2, other arithmetic, gate_half(): (u[here].astype(jnp.float32) * slope).astype(jnp.bfloat16)  5.12 us
    all_to_all x3, waiting for transfers between devices, across(): lax.all_to_all(block, 'replica', split_axis=0, concat_axis=0, tiled=True)  4.77 us
  transfers between devices with their start and end apart: 29, of which 13 were waited for; matrix products, arithmetic and copies ran while one was open for 15% of the time, Pallas kernels for 19%

profile of v2, /device:TPU:2, one launch (start us, length us, event | category | flops | bytes accessed | tf_op | source)
XLA Modules:
  0.0 190.2 jit_solution(18290400060230421254)
XLA Ops:
  2.0 3.7 %shard_map.85 = f32[512,1280]{1,0:T(8,128)S(1)} custom-call(s32[1]{0:T(128)S(6)} %sub.35.half_ref, bf16[512,1280]{1,0:T(8,128)(2,1)S(1)} %bitcast.102, bf16[1280,2560]{1,0:T(8,128)(2,1)} %bitcast.113), custom_call_target="tpu_custom_call" | custom-call | flops 1024 | bytes 1024 | tf_op jit(solution)/shard_map/pallas_call | solution.py:43
  8.9 4.8 %collective-permute-start = (s32[1,17]{1,0:T(1,128)S(1)}, s32[1,17]{1,0:T(1,128)S(1)}, u32[]{:S(2)}, u32[]{:S(2)}) collective-permute-start(s32[1,17]{1,0:T(1,128)S(1)} %add_bitcast_fusion), channel_id=1, source_target_pairs={{0,32},{32,64},{64,96},{96,128},{128,160},{160,192},{192,224},{1,3... | collective-permute-start | bytes 212 | tf_op jit(solution)/shard_map/ppermute | solution.py:16
  14.8 4.7 %shard_map.86 = f32[512,1280]{1,0:T(8,128)} custom-call(s32[1]{0:T(128)} %bitcast.3.half_ref.refs_0_, bf16[512,1280]{1,0:T(8,128)(2,1)S(1)} %bitcast.103, bf16[1280,2560]{1,0:T(8,128)(2,1)} %bitcast.114), custom_call_target="tpu_custom_call" | custom-call | flops 1024 | bytes 1024 | tf_op jit(solution)/shard_map/pallas_call | solution.py:43
  21.1 3.4 %collective-permute-done.1 = f16[256,1280]{1,0:T(8,128)(2,1)} collective-permute-done((f16[256,1280]{1,0:T(8,128)(2,1)}, f16[256,1280]{1,0:T(8,128)(2,1)}, u32[]{:S(2)}, u32[]{:S(2)}) %collective-permute-start.1) | collective-permute-done | bytes 655392 | tf_op jit(solution)/shard_map/ppermute | solution.py:20
  24.5 2.9 %multiply_convert_fusion.3.refs_1_.ga_ref = bf16[256,1280]{1,0:T(8,128)(2,1)} fusion(f16[256,1280]{1,0:T(8,128)(2,1)} %collective-permute-done.1, f32[512,1280]{1,0:T(8,128)} %shard_map.86, bf16[512,1280]{1,0:T(8,128)(2,1)S(1)} %bitcast.98), kind=kLoop, calls=%fused_computation.3 | loop fusion | flops 4259840 | bytes 3276800 | tf_op jit(solution)/shard_map/convert_element_type | solution.py:332
  31.3 8.6 %all-to-all-start = ((bf16[16,1,2]{2,1,0:T(2,128)(2,1)}), bf16[16,1,2]{2,1,0:T(2,128)(2,1)S(1)}, u32[]{:S(2)}, u32[]{:S(2)}) async-start(bf16[16,1,2]{2,1,0:T(2,128)(2,1)} %reshape.155), calls=%async_computation | async-start | bytes 16384 | tf_op jit(solution)/shard_map/all_to_all | solution.py:339
  42.6 4.8 %all-to-all-done = bf16[16,1,2]{2,1,0:T(2,128)(2,1)S(1)} async-done(((bf16[16,1,2]{2,1,0:T(2,128)(2,1)}), bf16[16,1,2]{2,1,0:T(2,128)(2,1)S(1)}, u32[]{:S(2)}, u32[]{:S(2)}) %all-to-all-start) | async-done | bytes 96 | tf_op jit(solution)/shard_map/all_to_all | solution.py:339
  47.8 2.9 %shard_map.87 = f32[256,1280]{1,0:T(8,128)S(1)} custom-call(s32[1]{0:T(128)S(6)} %sub.35.half_ref, bf16[256,1280]{1,0:T(8,128)(2,1)S(1)} %bitcast.105, bf16[1280,2560]{1,0:T(8,128)(2,1)} %bitcast.115), custom_call_target="tpu_custom_call" | custom-call | flops 1024 | bytes 1024 | tf_op jit(solution)/shard_map/pallas_call | solution.py:43
  52.3 3.6 %shard_map.88 = f32[256,1280]{1,0:T(8,128)} custom-call(s32[1]{0:T(128)} %bitcast.3.half_ref.refs_0_, bf16[256,1280]{1,0:T(8,128)(2,1)S(1)} %bitcast.106, bf16[1280,2560]{1,0:T(8,128)(2,1)} %bitcast.116), custom_call_target="tpu_custom_call" | custom-call | flops 1024 | bytes 1024 | tf_op jit(solution)/shard_map/pallas_call | solution.py:43
  56.0 6.2 %shard_map.89.refs_6_ = bf16[512,1280]{1,0:T(8,128)(2,1)} custom-call(s32[1]{0:T(128)} %bitcast.3.half_ref.refs_0_, bf16[256,1280]{1,0:T(8,128)(2,1)} %multiply_convert_fusion.3.refs_1_.ga_ref, bf16[256,1280]{1,0:T(8,128)(2,1)} %collective-permute-done.5.refs_2_.ga_ref, bf16[1280,2560]{1,0:T(8,128)(2,1)} %bitcast.117, bf16[512,1280]{1,0:T(8,128)(2,1)S(1)} %bitcast.100, ...), custom_call_target="tpu_custom_call" | custom-call | flops 1024 | bytes 1024 | tf_op jit(solution)/shard_map/pallas_call | solution.py:43
  62.2 5.1 %shard_map.90 = (bf16[640,1280]{1,0:T(8,128)(2,1)}, f32[640,1280]{1,0:T(8,128)}) custom-call(bf16[640,512]{1,0:T(8,128)(2,1)S(1)} %bitcast.110, bf16[640,512]{1,0:T(8,128)(2,1)S(1)} %bitcast.108, bf16[256,1280]{1,0:T(8,128)(2,1)} %multiply_convert_fusion.3.refs_1_.ga_ref, bf16[256,1280]{1,0:T(8,128)(2,1)S(1)} %multiply_convert_fusion.2.gb_ref.refs_1_, ...), custom_call_target="tpu_custom_call" | custom-call | flops 1024 | bytes 1024 | tf_op jit(solution)/shard_map/pallas_call | solution.py:43
  67.4 5.9 %shard_map.91 = bf16[512,1280]{1,0:T(8,128)(2,1)} custom-call(s32[1]{0:T(128)} %bitcast.3.half_ref.refs_0_, bf16[256,1280]{1,0:T(8,128)(2,1)S(1)} %multiply_convert_fusion.2.gb_ref.refs_1_, bf16[256,1280]{1,0:T(8,128)(2,1)} %collective-permute-done.4.refs_2_.gb_ref, bf16[1280,2560]{1,0:T(8,128)(2,1)} %bitcast.118, ...), custom_call_target="tpu_custom_call", output_to_operand_aliasing={{}: (6, {})} | custom-call | flops 1024 | bytes 1024 | tf_op jit(solution)/shard_map/pallas_call | solution.py:43
  73.3 7.9 %all-to-all-start.2 = ((bf16[16,2,16,1280]{3,2,1,0:T(8,128)(2,1)}), bf16[16,2,16,1280]{3,2,1,0:T(8,128)(2,1)S(1)}, u32[]{:S(2)}, u32[]{:S(2)}) async-start(bf16[16,2,16,1280]{3,2,1,0:T(8,128)(2,1)} %bitcast.119), calls=%async_computation.2 | async-start | bytes 2621440 | tf_op jit(solution)/shard_map/all_to_all | solution.py:339
  81.3 2.9 %multiply_convert_fusion = bf16[256,1280]{1,0:T(8,128)(2,1)} fusion(f32[256,1280]{1,0:T(8,128)} %shard_map.88, f16[256,1280]{1,0:T(8,128)(2,1)} %collective-permute-done.3, bf16[256,1280]{1,0:T(8,128)(2,1)S(1)} %bitcast.107, f32[256]{0:T(256)S(1)} %mul.76), kind=kLoop, calls=%fused_computation | loop fusion | flops 3604480 | bytes 3277824 | tf_op jit(solution)/shard_map/convert_element_type | solution.py:382
  84.2 5.3 %shard_map.92 = (bf16[640,1280]{1,0:T(8,128)(2,1)}, f32[640,1280]{1,0:T(8,128)}) custom-call(bf16[640,512]{1,0:T(8,128)(2,1)S(1)} %bitcast.111, bf16[640,512]{1,0:T(8,128)(2,1)S(1)} %bitcast.109, bf16[256,1280]{1,0:T(8,128)(2,1)} %collective-permute-done.5.refs_2_.ga_ref, bf16[256,1280]{1,0:T(8,128)(2,1)} %collective-permute-done.4.refs_2_.gb_ref, ...), custom_call_target="tpu_custom_call" | custom-call | flops 1024 | bytes 1024 | tf_op jit(solution)/shard_map/pallas_call | solution.py:43
  90.0 5.1 %collective-permute-start.6 = (bf16[16,16,1280]{2,1,0:T(8,128)(2,1)}, bf16[16,16,1280]{2,1,0:T(8,128)(2,1)S(1)}, u32[]{:S(2)}, u32[]{:S(2)}) collective-permute-start(bf16[16,16,1280]{2,1,0:T(8,128)(2,1)} %bitcast.133), channel_id=1, source_target_pairs={{0,32},{32,64},{64,96},{96,128},{128,160},{160,192},{192,224},{1,3... | collective-permute-start | bytes 1966088 | tf_op jit(solution)/shard_map/ppermute | solution.py:16
  96.8 3.9 %collective-permute-start.10 = (bf16[80,640]{1,0:T(8,128)(2,1)}, bf16[80,640]{1,0:T(8,128)(2,1)}, u32[]{:S(2)}, u32[]{:S(2)}) collective-permute-start(bf16[80,640]{1,0:T(8,128)(2,1)} %get-tuple-element.162), channel_id=1, source_target_pairs={{0,28},{2,30},{4,0},{6,2},{8,4},{10,6},{12,8},{14,10},{16,12},{18,... | collective-permute-start | bytes 307208 | tf_op jit(solution)/shard_map/ppermute | solution.py:29
  102.7 8.6 %collective-permute-done.6.x_ref = bf16[16,16,1280]{2,1,0:T(8,128)(2,1)S(1)} collective-permute-done((bf16[16,16,1280]{2,1,0:T(8,128)(2,1)}, bf16[16,16,1280]{2,1,0:T(8,128)(2,1)S(1)}, u32[]{:S(2)}, u32[]{:S(2)}) %collective-permute-start.6) | collective-permute-done | bytes 655392 | tf_op jit(solution)/shard_map/ppermute | solution.py:16
  111.3 4.0 %collective-permute-start.14 = (bf16[80,640]{1,0:T(8,128)(2,1)}, bf16[80,640]{1,0:T(8,128)(2,1)}, u32[]{:S(2)}, u32[]{:S(2)}) collective-permute-start(bf16[80,640]{1,0:T(8,128)(2,1)} %get-tuple-element.160), channel_id=1, source_target_pairs={{0,28},{2,30},{4,0},{6,2},{8,4},{10,6},{12,8},{14,10},{16,12},{18,... | collective-permute-start | bytes 307208 | tf_op jit(solution)/shard_map/ppermute | solution.py:29
  117.3 5.2 %all-to-all-start.1 = ((bf16[16,2,16,1280]{3,2,1,0:T(8,128)(2,1)}), bf16[16,2,16,1280]{3,2,1,0:T(8,128)(2,1)S(1)}, u32[]{:S(2)}, u32[]{:S(2)}) async-start(bf16[16,2,16,1280]{3,2,1,0:T(8,128)(2,1)} %bitcast.23), calls=%async_computation.1 | async-start | bytes 2621440 | tf_op jit(solution)/shard_map/all_to_all | solution.py:339
  123.2 4.2 %collective-permute-start.9 = (bf16[16,16,1280]{2,1,0:T(8,128)(2,1)S(1)}, bf16[16,16,1280]{2,1,0:T(8,128)(2,1)S(1)}, u32[]{:S(2)}, u32[]{:S(2)}) collective-permute-start(bf16[16,16,1280]{2,1,0:T(8,128)(2,1)S(1)} %shard_map.94), channel_id=1, source_target_pairs={{32,0},{64,32},{96,64},{128,96},{160,128},{192,160},{224,192},{33,... | collective-permute-start | bytes 1966088 | tf_op jit(solution)/shard_map/ppermute | solution.py:16
  135.7 22.9 %collective-permute-done.12 = bf16[80,1280]{1,0:T(8,128)(2,1)S(1)} collective-permute-done((bf16[80,1280]{1,0:T(8,128)(2,1)S(1)}, bf16[80,1280]{1,0:T(8,128)(2,1)S(1)}, u32[]{:S(2)}, u32[]{:S(2)}) %collective-permute-start.12) | collective-permute-done | bytes 204832 | tf_op jit(solution)/shard_map/ppermute | solution.py:29
  169.0 2.7 %collective-permute-done.16 = bf16[80,1280]{1,0:T(8,128)(2,1)S(1)} collective-permute-done((bf16[80,1280]{1,0:T(8,128)(2,1)S(1)}, bf16[80,1280]{1,0:T(8,128)(2,1)S(1)}, u32[]{:S(2)}, u32[]{:S(2)}) %collective-permute-start.16) | collective-permute-done | bytes 204832 | tf_op jit(solution)/shard_map/ppermute | solution.py:29
  180.7 2.9 %collective-permute-done.20 = bf16[80,1280]{1,0:T(8,128)(2,1)S(1)} collective-permute-done((bf16[80,1280]{1,0:T(8,128)(2,1)S(1)}, bf16[80,1280]{1,0:T(8,128)(2,1)S(1)}, u32[]{:S(2)}, u32[]{:S(2)}) %collective-permute-start.20) | collective-permute-done | bytes 204832 | tf_op jit(solution)/shard_map/ppermute | solution.py:29
  (107 shorter events, 56.5 us)
Async XLA Ops:
  6.6 17.9 %collective-permute-start.1 = (f16[256,1280]{1,0:T(8,128)(2,1)}, f16[256,1280]{1,0:T(8,128)(2,1)}, u32[]{:S(2)}, u32[]{:S(2)}) collective-permute-start(f16[256,1280]{1,0:T(8,128)(2,1)} %multiply_convert_fusion.5), channel_id=1, source_target_pairs={{0,1},{1,0},{2,3},{3,2},{4,5},{5,4},{6,7},{7,6},{8,9},{9,8},{10,11... | collective-permute-start | bytes 1966088 | tf_op jit(solution)/shard_map/ppermute | solution.py:20
  8.9 20.2 %collective-permute-start = (s32[1,17]{1,0:T(1,128)S(1)}, s32[1,17]{1,0:T(1,128)S(1)}, u32[]{:S(2)}, u32[]{:S(2)}) collective-permute-start(s32[1,17]{1,0:T(1,128)S(1)} %add_bitcast_fusion), channel_id=1, source_target_pairs={{0,32},{32,64},{64,96},{96,128},{128,160},{160,192},{192,224},{1,3... | collective-permute-start | bytes 212 | tf_op jit(solution)/shard_map/ppermute | solution.py:16
  14.7 25.2 %collective-permute-start.2 = (f16[256,1280]{1,0:T(8,128)(2,1)}, f16[256,1280]{1,0:T(8,128)(2,1)}, u32[]{:S(2)}, u32[]{:S(2)}) collective-permute-start(f16[256,1280]{1,0:T(8,128)(2,1)} %multiply_convert_fusion.4), channel_id=1, source_target_pairs={{0,1},{1,0},{2,3},{3,2},{4,5},{5,4},{6,7},{7,6},{8,9},{9,8},{10,11... | collective-permute-start | bytes 1966088 | tf_op jit(solution)/shard_map/ppermute | solution.py:20
  27.5 28.5 %collective-permute-start.5 = (bf16[256,1280]{1,0:T(8,128)(2,1)}, bf16[256,1280]{1,0:T(8,128)(2,1)}, u32[]{:S(2)}, u32[]{:S(2)}) collective-permute-start(bf16[256,1280]{1,0:T(8,128)(2,1)} %multiply_convert_fusion.3.refs_1_.ga_ref), channel_id=1, source_target_pairs={{0,1},{1,0},{2,3},{3,2},{4,5},{5,4},{6,7},{7,6},{8,9},{9,8},{10,11... | collective-permute-start | bytes 1966088 | tf_op jit(solution)/shard_map/ppermute | solution.py:20
  31.3 16.1 %all-to-all-start = ((bf16[16,1,2]{2,1,0:T(2,128)(2,1)}), bf16[16,1,2]{2,1,0:T(2,128)(2,1)S(1)}, u32[]{:S(2)}, u32[]{:S(2)}) async-start(bf16[16,1,2]{2,1,0:T(2,128)(2,1)} %reshape.155), calls=%async_computation | async-start | bytes 16384 | tf_op jit(solution)/shard_map/all_to_all | solution.py:339
  42.1 25.2 %collective-permute-start.4 = (bf16[256,1280]{1,0:T(8,128)(2,1)S(1)}, bf16[256,1280]{1,0:T(8,128)(2,1)}, u32[]{:S(2)}, u32[]{:S(2)}) collective-permute-start(bf16[256,1280]{1,0:T(8,128)(2,1)S(1)} %multiply_convert_fusion.2.gb_ref.refs_1_), channel_id=1, source_target_pairs={{0,1},{1,0},{2,3},{3,2},{4,5},{5,4},{6,7},{7,6},{8,9},{9,8},{10,11... | collective-permute-start | bytes 1966088 | tf_op jit(solution)/shard_map/ppermute | solution.py:20
  51.6 29.6 %collective-permute-start.3 = (f16[256,1280]{1,0:T(8,128)(2,1)}, f16[256,1280]{1,0:T(8,128)(2,1)}, u32[]{:S(2)}, u32[]{:S(2)}) collective-permute-start(f16[256,1280]{1,0:T(8,128)(2,1)} %multiply_convert_fusion.1), channel_id=1, source_target_pairs={{0,1},{1,0},{2,3},{3,2},{4,5},{5,4},{6,7},{7,6},{8,9},{9,8},{10,11... | collective-permute-start | bytes 1966088 | tf_op jit(solution)/shard_map/ppermute | solution.py:20
  67.3 27.7 %collective-permute-start.8 = (bf16[8,80,1280]{2,1,0:T(8,128)(2,1)}, bf16[8,80,1280]{2,1,0:T(8,128)(2,1)}, u32[]{:S(2)}, u32[]{:S(2)}) collective-permute-start(bf16[8,80,1280]{2,1,0:T(8,128)(2,1)} %bitcast.138), channel_id=1, source_target_pairs={{0,2},{2,0},{4,6},{6,4},{8,10},{10,8},{12,14},{14,12},{16,18},{18,... | collective-permute-start | bytes 4915208 | tf_op jit(solution)/shard_map/ppermute | solution.py:24
  73.3 43.9 %all-to-all-start.2 = ((bf16[16,2,16,1280]{3,2,1,0:T(8,128)(2,1)}), bf16[16,2,16,1280]{3,2,1,0:T(8,128)(2,1)S(1)}, u32[]{:S(2)}, u32[]{:S(2)}) async-start(bf16[16,2,16,1280]{3,2,1,0:T(8,128)(2,1)} %bitcast.119), calls=%async_computation.2 | async-start | bytes 2621440 | tf_op jit(solution)/shard_map/all_to_all | solution.py:339
  89.5 11.2 %collective-permute-start.7 = (bf16[8,80,1280]{2,1,0:T(8,128)(2,1)}, bf16[8,80,1280]{2,1,0:T(8,128)(2,1)S(1)}, u32[]{:S(2)}, u32[]{:S(2)}) collective-permute-start(bf16[8,80,1280]{2,1,0:T(8,128)(2,1)} %bitcast.139), channel_id=1, source_target_pairs={{0,2},{2,0},{4,6},{6,4},{8,10},{10,8},{12,14},{14,12},{16,18},{18,... | collective-permute-start | bytes 4915208 | tf_op jit(solution)/shard_map/ppermute | solution.py:24
  90.0 21.3 %collective-permute-start.6 = (bf16[16,16,1280]{2,1,0:T(8,128)(2,1)}, bf16[16,16,1280]{2,1,0:T(8,128)(2,1)S(1)}, u32[]{:S(2)}, u32[]{:S(2)}) collective-permute-start(bf16[16,16,1280]{2,1,0:T(8,128)(2,1)} %bitcast.133), channel_id=1, source_target_pairs={{0,32},{32,64},{64,96},{96,128},{128,160},{160,192},{192,224},{1,3... | collective-permute-start | bytes 1966088 | tf_op jit(solution)/shard_map/ppermute | solution.py:16
  96.8 30.5 %collective-permute-start.10 = (bf16[80,640]{1,0:T(8,128)(2,1)}, bf16[80,640]{1,0:T(8,128)(2,1)}, u32[]{:S(2)}, u32[]{:S(2)}) collective-permute-start(bf16[80,640]{1,0:T(8,128)(2,1)} %get-tuple-element.162), channel_id=1, source_target_pairs={{0,28},{2,30},{4,0},{6,2},{8,4},{10,6},{12,8},{14,10},{16,12},{18,... | collective-permute-start | bytes 307208 | tf_op jit(solution)/shard_map/ppermute | solution.py:29
  100.7 26.6 %collective-permute-start.11 = (bf16[80,640]{1,0:T(8,128)(2,1)S(1)}, bf16[80,640]{1,0:T(8,128)(2,1)}, u32[]{:S(2)}, u32[]{:S(2)}) collective-permute-start(bf16[80,640]{1,0:T(8,128)(2,1)S(1)} %get-tuple-element.161), channel_id=1, source_target_pairs={{0,4},{2,6},{4,8},{6,10},{8,12},{10,14},{12,16},{14,18},{16,20},{1... | collective-permute-start | bytes 307208 | tf_op jit(solution)/shard_map/ppermute | solution.py:29
  111.3 19.6 %collective-permute-start.14 = (bf16[80,640]{1,0:T(8,128)(2,1)}, bf16[80,640]{1,0:T(8,128)(2,1)}, u32[]{:S(2)}, u32[]{:S(2)}) collective-permute-start(bf16[80,640]{1,0:T(8,128)(2,1)} %get-tuple-element.160), channel_id=1, source_target_pairs={{0,28},{2,30},{4,0},{6,2},{8,4},{10,6},{12,8},{14,10},{16,12},{18,... | collective-permute-start | bytes 307208 | tf_op jit(solution)/shard_map/ppermute | solution.py:29
  115.3 15.7 %collective-permute-start.15 = (bf16[80,640]{1,0:T(8,128)(2,1)S(1)}, bf16[80,640]{1,0:T(8,128)(2,1)}, u32[]{:S(2)}, u32[]{:S(2)}) collective-permute-start(bf16[80,640]{1,0:T(8,128)(2,1)S(1)} %get-tuple-element.159), channel_id=1, source_target_pairs={{0,4},{2,6},{4,8},{6,10},{8,12},{10,14},{12,16},{14,18},{16,20},{1... | collective-permute-start | bytes 307208 | tf_op jit(solution)/shard_map/ppermute | solution.py:29
  117.3 70.8 %all-to-all-start.1 = ((bf16[16,2,16,1280]{3,2,1,0:T(8,128)(2,1)}), bf16[16,2,16,1280]{3,2,1,0:T(8,128)(2,1)S(1)}, u32[]{:S(2)}, u32[]{:S(2)}) async-start(bf16[16,2,16,1280]{3,2,1,0:T(8,128)(2,1)} %bitcast.23), calls=%async_computation.1 | async-start | bytes 2621440 | tf_op jit(solution)/shard_map/all_to_all | solution.py:339
  123.2 64.8 %collective-permute-start.9 = (bf16[16,16,1280]{2,1,0:T(8,128)(2,1)S(1)}, bf16[16,16,1280]{2,1,0:T(8,128)(2,1)S(1)}, u32[]{:S(2)}, u32[]{:S(2)}) collective-permute-start(bf16[16,16,1280]{2,1,0:T(8,128)(2,1)S(1)} %shard_map.94), channel_id=1, source_target_pairs={{32,0},{64,32},{96,64},{128,96},{160,128},{192,160},{224,192},{33,... | collective-permute-start | bytes 1966088 | tf_op jit(solution)/shard_map/ppermute | solution.py:16
  128.9 30.8 %collective-permute-start.13 = (bf16[80,1280]{1,0:T(8,128)(2,1)S(1)}, bf16[80,1280]{1,0:T(8,128)(2,1)S(1)}, u32[]{:S(2)}, u32[]{:S(2)}) collective-permute-start(bf16[80,1280]{1,0:T(8,128)(2,1)S(1)} %get-tuple-element.155), channel_id=1, source_target_pairs={{0,4},{2,6},{4,8},{6,10},{8,12},{10,14},{12,16},{14,18},{16,20},{1... | collective-permute-start | bytes 614408 | tf_op jit(solution)/shard_map/ppermute | solution.py:29
  130.9 27.7 %collective-permute-start.12 = (bf16[80,1280]{1,0:T(8,128)(2,1)S(1)}, bf16[80,1280]{1,0:T(8,128)(2,1)S(1)}, u32[]{:S(2)}, u32[]{:S(2)}) collective-permute-start(bf16[80,1280]{1,0:T(8,128)(2,1)S(1)} %get-tuple-element.156), channel_id=1, source_target_pairs={{0,28},{2,30},{4,0},{6,2},{8,4},{10,6},{12,8},{14,10},{16,12},{18,... | collective-permute-start | bytes 614408 | tf_op jit(solution)/shard_map/ppermute | solution.py:29
  133.6 28.9 %collective-permute-start.18 = (bf16[80,1280]{1,0:T(8,128)(2,1)S(1)}, bf16[80,1280]{1,0:T(8,128)(2,1)S(1)}, u32[]{:S(2)}, u32[]{:S(2)}) collective-permute-start(bf16[80,1280]{1,0:T(8,128)(2,1)S(1)} %get-tuple-element.151), channel_id=1, source_target_pairs={{0,28},{2,30},{4,0},{6,2},{8,4},{10,6},{12,8},{14,10},{16,12},{18,... | collective-permute-start | bytes 614408 | tf_op jit(solution)/shard_map/ppermute | solution.py:29
  135.6 28.1 %collective-permute-start.19 = (bf16[80,1280]{1,0:T(8,128)(2,1)S(1)}, bf16[80,1280]{1,0:T(8,128)(2,1)S(1)}, u32[]{:S(2)}, u32[]{:S(2)}) collective-permute-start(bf16[80,1280]{1,0:T(8,128)(2,1)S(1)} %get-tuple-element.152), channel_id=1, source_target_pairs={{0,4},{2,6},{4,8},{6,10},{8,12},{10,14},{12,16},{14,18},{16,20},{1... | collective-permute-start | bytes 614408 | tf_op jit(solution)/shard_map/ppermute | solution.py:29
  160.9 10.7 %collective-permute-start.17 = (bf16[80,1280]{1,0:T(8,128)(2,1)S(1)}, bf16[80,1280]{1,0:T(8,128)(2,1)S(1)}, u32[]{:S(2)}, u32[]{:S(2)}) collective-permute-start(bf16[80,1280]{1,0:T(8,128)(2,1)S(1)} %get-tuple-element.153), channel_id=1, source_target_pairs={{0,4},{2,6},{4,8},{6,10},{8,12},{10,14},{12,16},{14,18},{16,20},{1... | collective-permute-start | bytes 614408 | tf_op jit(solution)/shard_map/ppermute | solution.py:29
  168.4 8.3 %collective-permute-start.23 = (bf16[80,1280]{1,0:T(8,128)(2,1)S(1)}, bf16[80,1280]{1,0:T(8,128)(2,1)S(1)}, u32[]{:S(2)}, u32[]{:S(2)}) collective-permute-start(bf16[80,1280]{1,0:T(8,128)(2,1)S(1)} %get-tuple-element.148), channel_id=1, source_target_pairs={{0,4},{2,6},{4,8},{6,10},{8,12},{10,14},{12,16},{14,18},{16,20},{1... | collective-permute-start | bytes 614408 | tf_op jit(solution)/shard_map/ppermute | solution.py:29
  172.8 10.8 %collective-permute-start.21 = (bf16[80,1280]{1,0:T(8,128)(2,1)S(1)}, bf16[80,1280]{1,0:T(8,128)(2,1)S(1)}, u32[]{:S(2)}, u32[]{:S(2)}) collective-permute-start(bf16[80,1280]{1,0:T(8,128)(2,1)S(1)} %get-tuple-element.149), channel_id=1, source_target_pairs={{0,4},{2,6},{4,8},{6,10},{8,12},{10,14},{12,16},{14,18},{16,20},{1... | collective-permute-start | bytes 614408 | tf_op jit(solution)/shard_map/ppermute | solution.py:29
  (16 other events, 127.7 us)

commit v3 on v2

--- a/solution.py
+++ b/solution.py
@@ -224,6 +224,14 @@
 def pick(index, x):
     shape = shaped((index.shape[0],) + x.shape[1:], x.dtype)
     return kernel(pick_body, shape, (index, x), (pltpu.SMEM, pltpu.VMEM))
+
+
+def settle_body(x_ref, o_ref):
+    pltpu.sync_copy(x_ref, o_ref)
+
+
+def settle(x):
+    return kernel(settle_body, pltpu.HBM(x.shape, x.dtype), (x,), (pltpu.VMEM,), (), pltpu.HBM)
 
 
 class Order:
@@ -388,16 +396,23 @@
     ring_nbr.round()
     (outputs,) = order.tie(outputs)
     packed = order.mark(pick(source, outputs))
-    arrived = across(packed.reshape(replicas, cap, tokens, width))
     (back,) = order.tie(back)
     returned = order.mark(pick(place, back.reshape(recv, tokens, width)))
     returned = shift(returned, "section", -1)
+    sent = order.here(ring_own.down, ring_own.up, ring_nbr.down, ring_nbr.up)
+    ring_own.down, ring_own.up, ring_nbr.down, ring_nbr.up = sent
+    (packed,) = order.tie(packed)
+    arrived = across(packed.reshape(replicas, cap, tokens, width))
     ring_own.round()
     ring_nbr.round()
     ring_own.round()
     ring_nbr.round()
+    (x,) = order.tie(returned)
+    returned = order.mark(settle(x))
     ring_own.round()
     ring_nbr.round()
+    (x,) = order.tie(arrived)
+    arrived = order.mark(settle(x))
     sum_own = ring_own.round()
     sum_nbr = ring_nbr.round()
     zero = jnp.zeros((), jnp.int32)

time: 191 us -> 190 us (level)
  Pallas kernels: 39.9 us -> 41.9 us
    pallas_call x10 -> x12, Pallas kernels: 39.9 us -> 41.9 us  [kernel(): pl.pallas_call(body, in_specs=[pl.BlockSpec(memory_space=space) for space...]
    convert_element_type x3 -> x4, other arithmetic: 3.82 us -> 5.18 us  [round(): sent = self.term(self.keep, self.got, -k, down).astype(jnp.bfloat16)]
    convert_element_type x3 -> x2, other arithmetic: 3.91 us -> 2.6 us  [round(): sent = self.term(self.keep, self.got, k, up).astype(jnp.bfloat16)]
  transfers between devices with their start and end apart: 29 -> 29, of which waited for: 13 -> 17; matrix products, arithmetic and copies ran while one was open for 15% -> 14% of each run, Pallas kernels for 19% -> 20%
where the time goes in v3:
time: 190 us; the launch traced here: 189 us
  starting transfers between devices  60.2 us (32%)
  waiting for transfers between devices  54.5 us (29%)
  Pallas kernels  41.9 us (22%)
  other arithmetic  24.4 us (13%)
  local copies, waits for them, and re-layouts  6.6 us (3%)
    pallas_call x12, Pallas kernels, kernel(): pl.pallas_call(body, in_specs=[pl.BlockSpec(memory_space=space) for space...  41.9 us
    ppermute x16, waiting for transfers between devices, round_chips(): lax.ppermute(block, 'replica', [(r, (r + 2 * distance) % size) for r in r...  38.6 us
    all_to_all x3, starting transfers between devices, across(): lax.all_to_all(block, 'replica', split_axis=0, concat_axis=0, tiled=True)  21.2 us
    ppermute x16, starting transfers between devices, round_chips(): lax.ppermute(block, 'replica', [(r, (r + 2 * distance) % size) for r in r...  19.1 us
    ppermute x3, starting transfers between devices, shift(): return lax.ppermute(block, axis, route)  15 us
    ppermute x3, waiting for transfers between devices, shift(): return lax.ppermute(block, axis, route)  6.9 us
    all_to_all x3, waiting for transfers between devices, across(): lax.all_to_all(block, 'replica', split_axis=0, concat_axis=0, tiled=True)  5.59 us
    convert_element_type x4, other arithmetic, round(): sent = self.term(self.keep, self.got, -k, down).astype(jnp.bfloat16)  5.18 us
  transfers between devices with their start and end apart: 29, of which 17 were waited for; matrix products, arithmetic and copies ran while one was open for 14% of the time, Pallas kernels for 20%

profile of v3, /device:TPU:2, one launch (start us, length us, event | category | flops | bytes accessed | tf_op | source)
XLA Modules:
  0.0 189.3 jit_solution(11763854551908034250)
XLA Ops:
  2.0 3.7 %shard_map.85 = f32[512,1280]{1,0:T(8,128)S(1)} custom-call(s32[1]{0:T(128)S(6)} %sub.35.half_ref, bf16[512,1280]{1,0:T(8,128)(2,1)S(1)} %bitcast.102, bf16[1280,2560]{1,0:T(8,128)(2,1)} %bitcast.113), custom_call_target="tpu_custom_call" | custom-call | flops 1024 | bytes 1024 | tf_op jit(solution)/shard_map/pallas_call | solution.py:43
  8.9 4.8 %collective-permute-start = (s32[1,17]{1,0:T(1,128)S(1)}, s32[1,17]{1,0:T(1,128)S(1)}, u32[]{:S(2)}, u32[]{:S(2)}) collective-permute-start(s32[1,17]{1,0:T(1,128)S(1)} %add_bitcast_fusion), channel_id=1, source_target_pairs={{0,32},{32,64},{64,96},{96,128},{128,160},{160,192},{192,224},{1,3... | collective-permute-start | bytes 212 | tf_op jit(solution)/shard_map/ppermute | solution.py:16
  14.8 4.7 %shard_map.86 = f32[512,1280]{1,0:T(8,128)} custom-call(s32[1]{0:T(128)} %bitcast.3.half_ref.refs_0_, bf16[512,1280]{1,0:T(8,128)(2,1)S(1)} %bitcast.103, bf16[1280,2560]{1,0:T(8,128)(2,1)} %bitcast.114), custom_call_target="tpu_custom_call" | custom-call | flops 1024 | bytes 1024 | tf_op jit(solution)/shard_map/pallas_call | solution.py:43
  21.2 3.4 %collective-permute-done.1 = f16[256,1280]{1,0:T(8,128)(2,1)} collective-permute-done((f16[256,1280]{1,0:T(8,128)(2,1)}, f16[256,1280]{1,0:T(8,128)(2,1)}, u32[]{:S(2)}, u32[]{:S(2)}) %collective-permute-start.1) | collective-permute-done | bytes 655392 | tf_op jit(solution)/shard_map/ppermute | solution.py:20
  24.6 2.9 %multiply_convert_fusion.3.refs_1_.ga_ref = bf16[256,1280]{1,0:T(8,128)(2,1)} fusion(f16[256,1280]{1,0:T(8,128)(2,1)} %collective-permute-done.1, f32[512,1280]{1,0:T(8,128)} %shard_map.86, bf16[512,1280]{1,0:T(8,128)(2,1)S(1)} %bitcast.98), kind=kLoop, calls=%fused_computation.3 | loop fusion | flops 4259840 | bytes 3276800 | tf_op jit(solution)/shard_map/convert_element_type | solution.py:340
  31.3 8.6 %all-to-all-start = ((bf16[16,1,2]{2,1,0:T(2,128)(2,1)}), bf16[16,1,2]{2,1,0:T(2,128)(2,1)S(1)}, u32[]{:S(2)}, u32[]{:S(2)}) async-start(bf16[16,1,2]{2,1,0:T(2,128)(2,1)} %reshape.155), calls=%async_computation | async-start | bytes 16384 | tf_op jit(solution)/shard_map/all_to_all | solution.py:347
  39.9 2.2 %multiply_convert_fusion.2.gb_ref.refs_1_ = bf16[256,1280]{1,0:T(8,128)(2,1)S(1)} fusion(f16[256,1280]{1,0:T(8,128)(2,1)} %collective-permute-done.2, f32[512,1280]{1,0:T(8,128)} %shard_map.86, bf16[512,1280]{1,0:T(8,128)(2,1)S(1)} %bitcast.99), kind=kLoop, calls=%fused_computation.2 | loop fusion | flops 4259840 | bytes 3276800 | tf_op jit(solution)/shard_map/convert_element_type | solution.py:340
  42.6 4.8 %all-to-all-done = bf16[16,1,2]{2,1,0:T(2,128)(2,1)S(1)} async-done(((bf16[16,1,2]{2,1,0:T(2,128)(2,1)}), bf16[16,1,2]{2,1,0:T(2,128)(2,1)S(1)}, u32[]{:S(2)}, u32[]{:S(2)}) %all-to-all-start) | async-done | bytes 96 | tf_op jit(solution)/shard_map/all_to_all | solution.py:347
  47.8 2.9 %shard_map.87 = f32[256,1280]{1,0:T(8,128)S(1)} custom-call(s32[1]{0:T(128)S(6)} %sub.35.half_ref, bf16[256,1280]{1,0:T(8,128)(2,1)S(1)} %bitcast.105, bf16[1280,2560]{1,0:T(8,128)(2,1)} %bitcast.115), custom_call_target="tpu_custom_call" | custom-call | flops 1024 | bytes 1024 | tf_op jit(solution)/shard_map/pallas_call | solution.py:43
  52.3 3.6 %shard_map.88 = f32[256,1280]{1,0:T(8,128)} custom-call(s32[1]{0:T(128)} %bitcast.3.half_ref.refs_0_, bf16[256,1280]{1,0:T(8,128)(2,1)S(1)} %bitcast.106, bf16[1280,2560]{1,0:T(8,128)(2,1)} %bitcast.116), custom_call_target="tpu_custom_call" | custom-call | flops 1024 | bytes 1024 | tf_op jit(solution)/shard_map/pallas_call | solution.py:43
  56.0 6.2 %shard_map.89.refs_6_ = bf16[512,1280]{1,0:T(8,128)(2,1)} custom-call(s32[1]{0:T(128)} %bitcast.3.half_ref.refs_0_, bf16[256,1280]{1,0:T(8,128)(2,1)} %multiply_convert_fusion.3.refs_1_.ga_ref, bf16[256,1280]{1,0:T(8,128)(2,1)} %collective-permute-done.5.refs_2_.ga_ref, bf16[1280,2560]{1,0:T(8,128)(2,1)} %bitcast.117, bf16[512,1280]{1,0:T(8,128)(2,1)S(1)} %bitcast.100, ...), custom_call_target="tpu_custom_call" | custom-call | flops 1024 | bytes 1024 | tf_op jit(solution)/shard_map/pallas_call | solution.py:43
  62.2 5.1 %shard_map.90 = (bf16[640,1280]{1,0:T(8,128)(2,1)}, f32[640,1280]{1,0:T(8,128)}) custom-call(bf16[640,512]{1,0:T(8,128)(2,1)S(1)} %bitcast.110, bf16[640,512]{1,0:T(8,128)(2,1)S(1)} %bitcast.108, bf16[256,1280]{1,0:T(8,128)(2,1)} %multiply_convert_fusion.3.refs_1_.ga_ref, bf16[256,1280]{1,0:T(8,128)(2,1)S(1)} %multiply_convert_fusion.2.gb_ref.refs_1_, ...), custom_call_target="tpu_custom_call" | custom-call | flops 1024 | bytes 1024 | tf_op jit(solution)/shard_map/pallas_call | solution.py:43
  67.4 5.9 %shard_map.91 = bf16[512,1280]{1,0:T(8,128)(2,1)} custom-call(s32[1]{0:T(128)} %bitcast.3.half_ref.refs_0_, bf16[256,1280]{1,0:T(8,128)(2,1)S(1)} %multiply_convert_fusion.2.gb_ref.refs_1_, bf16[256,1280]{1,0:T(8,128)(2,1)} %collective-permute-done.4.refs_2_.gb_ref, bf16[1280,2560]{1,0:T(8,128)(2,1)} %bitcast.118, ...), custom_call_target="tpu_custom_call", output_to_operand_aliasing={{}: (6, {})} | custom-call | flops 1024 | bytes 1024 | tf_op jit(solution)/shard_map/pallas_call | solution.py:43
  73.3 8.0 %all-to-all-start.1 = ((bf16[16,2,16,1280]{3,2,1,0:T(8,128)(2,1)}), bf16[16,2,16,1280]{3,2,1,0:T(8,128)(2,1)S(1)}, u32[]{:S(2)}, u32[]{:S(2)}) async-start(bf16[16,2,16,1280]{3,2,1,0:T(8,128)(2,1)} %bitcast.119), calls=%async_computation.1 | async-start | bytes 2621440 | tf_op jit(solution)/shard_map/all_to_all | solution.py:347
  81.3 2.9 %multiply_convert_fusion = bf16[256,1280]{1,0:T(8,128)(2,1)} fusion(f32[256,1280]{1,0:T(8,128)} %shard_map.88, f16[256,1280]{1,0:T(8,128)(2,1)} %collective-permute-done.3, bf16[256,1280]{1,0:T(8,128)(2,1)S(1)} %bitcast.107, f32[256]{0:T(256)S(1)} %mul.76), kind=kLoop, calls=%fused_computation | loop fusion | flops 3604480 | bytes 3277824 | tf_op jit(solution)/shard_map/convert_element_type | solution.py:390
  84.2 5.3 %shard_map.92 = (bf16[640,1280]{1,0:T(8,128)(2,1)}, f32[640,1280]{1,0:T(8,128)}) custom-call(bf16[640,512]{1,0:T(8,128)(2,1)S(1)} %bitcast.111, bf16[640,512]{1,0:T(8,128)(2,1)S(1)} %bitcast.109, bf16[256,1280]{1,0:T(8,128)(2,1)} %collective-permute-done.5.refs_2_.ga_ref, bf16[256,1280]{1,0:T(8,128)(2,1)} %collective-permute-done.4.refs_2_.gb_ref, ...), custom_call_target="tpu_custom_call" | custom-call | flops 1024 | bytes 1024 | tf_op jit(solution)/shard_map/pallas_call | solution.py:43
  90.0 5.1 %collective-permute-start.6 = (bf16[16,16,1280]{2,1,0:T(8,128)(2,1)}, bf16[16,16,1280]{2,1,0:T(8,128)(2,1)S(1)}, u32[]{:S(2)}, u32[]{:S(2)}) collective-permute-start(bf16[16,16,1280]{2,1,0:T(8,128)(2,1)} %bitcast.133), channel_id=1, source_target_pairs={{0,32},{32,64},{64,96},{96,128},{128,160},{160,192},{192,224},{1,3... | collective-permute-start | bytes 1966088 | tf_op jit(solution)/shard_map/ppermute | solution.py:16
  98.0 2.3 %collective-permute-start.9 = (bf16[80,640]{1,0:T(8,128)(2,1)S(1)}, bf16[80,640]{1,0:T(8,128)(2,1)}, u32[]{:S(2)}, u32[]{:S(2)}) collective-permute-start(bf16[80,640]{1,0:T(8,128)(2,1)S(1)} %get-tuple-element.176), channel_id=1, source_target_pairs={{0,28},{2,30},{4,0},{6,2},{8,4},{10,6},{12,8},{14,10},{16,12},{18,... | collective-permute-start | bytes 307208 | tf_op jit(solution)/shard_map/ppermute | solution.py:29
  104.3 6.9 %collective-permute-done.6.x_ref = bf16[16,16,1280]{2,1,0:T(8,128)(2,1)S(1)} collective-permute-done((bf16[16,16,1280]{2,1,0:T(8,128)(2,1)}, bf16[16,16,1280]{2,1,0:T(8,128)(2,1)S(1)}, u32[]{:S(2)}, u32[]{:S(2)}) %collective-permute-start.6) | collective-permute-done | bytes 655392 | tf_op jit(solution)/shard_map/ppermute | solution.py:16
  111.2 2.0 %shard_map.93 = bf16[32,16,1280]{2,1,0:T(8,128)(2,1)} custom-call(s32[32]{0:T(128)S(1)} %broadcast_add_fusion.index_ref, bf16[16,16,1280]{2,1,0:T(8,128)(2,1)S(1)} %collective-permute-done.6.x_ref), custom_call_target="tpu_custom_call" | custom-call | flops 1024 | bytes 1024 | tf_op jit(solution)/shard_map/pallas_call | solution.py:43
  118.1 4.7 %all-to-all-start.2 = ((bf16[16,2,16,1280]{3,2,1,0:T(8,128)(2,1)}), bf16[16,2,16,1280]{3,2,1,0:T(8,128)(2,1)S(1)}, u32[]{:S(2)}, u32[]{:S(2)}) async-start(bf16[16,2,16,1280]{3,2,1,0:T(8,128)(2,1)} %bitcast.25), calls=%async_computation.2 | async-start | bytes 2621440 | tf_op jit(solution)/shard_map/all_to_all | solution.py:347
  123.0 5.1 %collective-permute-start.21 = (bf16[16,16,1280]{2,1,0:T(8,128)(2,1)S(1)}, bf16[16,16,1280]{2,1,0:T(8,128)(2,1)S(1)}, u32[]{:S(2)}, u32[]{:S(2)}) collective-permute-start(bf16[16,16,1280]{2,1,0:T(8,128)(2,1)S(1)} %shard_map.94), channel_id=1, source_target_pairs={{32,0},{64,32},{96,64},{128,96},{160,128},{192,160},{224,192},{33,... | collective-permute-start | bytes 1966088 | tf_op jit(solution)/shard_map/ppermute | solution.py:16
  136.4 22.6 %collective-permute-done.15 = bf16[80,1280]{1,0:T(8,128)(2,1)S(1)} collective-permute-done((bf16[80,1280]{1,0:T(8,128)(2,1)S(1)}, bf16[80,1280]{1,0:T(8,128)(2,1)S(1)}, u32[]{:S(2)}, u32[]{:S(2)}) %collective-permute-start.15) | collective-permute-done | bytes 204832 | tf_op jit(solution)/shard_map/ppermute | solution.py:29
  175.0 2.2 %collective-permute-done.18 = bf16[80,1280]{1,0:T(8,128)(2,1)S(1)} collective-permute-done((bf16[80,1280]{1,0:T(8,128)(2,1)S(1)}, bf16[80,1280]{1,0:T(8,128)(2,1)S(1)}, u32[]{:S(2)}, u32[]{:S(2)}) %collective-permute-start.18) | collective-permute-done | bytes 204832 | tf_op jit(solution)/shard_map/ppermute | solution.py:29
  (107 shorter events, 61.9 us)
Async XLA Ops:
  6.6 17.9 %collective-permute-start.1 = (f16[256,1280]{1,0:T(8,128)(2,1)}, f16[256,1280]{1,0:T(8,128)(2,1)}, u32[]{:S(2)}, u32[]{:S(2)}) collective-permute-start(f16[256,1280]{1,0:T(8,128)(2,1)} %multiply_convert_fusion.5), channel_id=1, source_target_pairs={{0,1},{1,0},{2,3},{3,2},{4,5},{5,4},{6,7},{7,6},{8,9},{9,8},{10,11... | collective-permute-start | bytes 1966088 | tf_op jit(solution)/shard_map/ppermute | solution.py:20
  8.9 20.1 %collective-permute-start = (s32[1,17]{1,0:T(1,128)S(1)}, s32[1,17]{1,0:T(1,128)S(1)}, u32[]{:S(2)}, u32[]{:S(2)}) collective-permute-start(s32[1,17]{1,0:T(1,128)S(1)} %add_bitcast_fusion), channel_id=1, source_target_pairs={{0,32},{32,64},{64,96},{96,128},{128,160},{160,192},{192,224},{1,3... | collective-permute-start | bytes 212 | tf_op jit(solution)/shard_map/ppermute | solution.py:16
  14.7 25.2 %collective-permute-start.2 = (f16[256,1280]{1,0:T(8,128)(2,1)}, f16[256,1280]{1,0:T(8,128)(2,1)}, u32[]{:S(2)}, u32[]{:S(2)}) collective-permute-start(f16[256,1280]{1,0:T(8,128)(2,1)} %multiply_convert_fusion.4), channel_id=1, source_target_pairs={{0,1},{1,0},{2,3},{3,2},{4,5},{5,4},{6,7},{7,6},{8,9},{9,8},{10,11... | collective-permute-start | bytes 1966088 | tf_op jit(solution)/shard_map/ppermute | solution.py:20
  27.5 28.5 %collective-permute-start.5 = (bf16[256,1280]{1,0:T(8,128)(2,1)}, bf16[256,1280]{1,0:T(8,128)(2,1)}, u32[]{:S(2)}, u32[]{:S(2)}) collective-permute-start(bf16[256,1280]{1,0:T(8,128)(2,1)} %multiply_convert_fusion.3.refs_1_.ga_ref), channel_id=1, source_target_pairs={{0,1},{1,0},{2,3},{3,2},{4,5},{5,4},{6,7},{7,6},{8,9},{9,8},{10,11... | collective-permute-start | bytes 1966088 | tf_op jit(solution)/shard_map/ppermute | solution.py:20
  31.3 16.1 %all-to-all-start = ((bf16[16,1,2]{2,1,0:T(2,128)(2,1)}), bf16[16,1,2]{2,1,0:T(2,128)(2,1)S(1)}, u32[]{:S(2)}, u32[]{:S(2)}) async-start(bf16[16,1,2]{2,1,0:T(2,128)(2,1)} %reshape.155), calls=%async_computation | async-start | bytes 16384 | tf_op jit(solution)/shard_map/all_to_all | solution.py:347
  42.1 25.3 %collective-permute-start.4 = (bf16[256,1280]{1,0:T(8,128)(2,1)S(1)}, bf16[256,1280]{1,0:T(8,128)(2,1)}, u32[]{:S(2)}, u32[]{:S(2)}) collective-permute-start(bf16[256,1280]{1,0:T(8,128)(2,1)S(1)} %multiply_convert_fusion.2.gb_ref.refs_1_), channel_id=1, source_target_pairs={{0,1},{1,0},{2,3},{3,2},{4,5},{5,4},{6,7},{7,6},{8,9},{9,8},{10,11... | collective-permute-start | bytes 1966088 | tf_op jit(solution)/shard_map/ppermute | solution.py:20
  51.7 29.6 %collective-permute-start.3 = (f16[256,1280]{1,0:T(8,128)(2,1)}, f16[256,1280]{1,0:T(8,128)(2,1)}, u32[]{:S(2)}, u32[]{:S(2)}) collective-permute-start(f16[256,1280]{1,0:T(8,128)(2,1)} %multiply_convert_fusion.1), channel_id=1, source_target_pairs={{0,1},{1,0},{2,3},{3,2},{4,5},{5,4},{6,7},{7,6},{8,9},{9,8},{10,11... | collective-permute-start | bytes 1966088 | tf_op jit(solution)/shard_map/ppermute | solution.py:20
  67.3 27.8 %collective-permute-start.8 = (bf16[8,80,1280]{2,1,0:T(8,128)(2,1)}, bf16[8,80,1280]{2,1,0:T(8,128)(2,1)}, u32[]{:S(2)}, u32[]{:S(2)}) collective-permute-start(bf16[8,80,1280]{2,1,0:T(8,128)(2,1)} %bitcast.138), channel_id=1, source_target_pairs={{0,2},{2,0},{4,6},{6,4},{8,10},{10,8},{12,14},{14,12},{16,18},{18,... | collective-permute-start | bytes 4915208 | tf_op jit(solution)/shard_map/ppermute | solution.py:24
  73.3 40.7 %all-to-all-start.1 = ((bf16[16,2,16,1280]{3,2,1,0:T(8,128)(2,1)}), bf16[16,2,16,1280]{3,2,1,0:T(8,128)(2,1)S(1)}, u32[]{:S(2)}, u32[]{:S(2)}) async-start(bf16[16,2,16,1280]{3,2,1,0:T(8,128)(2,1)} %bitcast.119), calls=%async_computation.1 | async-start | bytes 2621440 | tf_op jit(solution)/shard_map/all_to_all | solution.py:347
  89.5 10.8 %collective-permute-start.7 = (bf16[8,80,1280]{2,1,0:T(8,128)(2,1)}, bf16[8,80,1280]{2,1,0:T(8,128)(2,1)S(1)}, u32[]{:S(2)}, u32[]{:S(2)}) collective-permute-start(bf16[8,80,1280]{2,1,0:T(8,128)(2,1)} %bitcast.139), channel_id=1, source_target_pairs={{0,2},{2,0},{4,6},{6,4},{8,10},{10,8},{12,14},{14,12},{16,18},{18,... | collective-permute-start | bytes 4915208 | tf_op jit(solution)/shard_map/ppermute | solution.py:24
  90.0 21.2 %collective-permute-start.6 = (bf16[16,16,1280]{2,1,0:T(8,128)(2,1)}, bf16[16,16,1280]{2,1,0:T(8,128)(2,1)S(1)}, u32[]{:S(2)}, u32[]{:S(2)}) collective-permute-start(bf16[16,16,1280]{2,1,0:T(8,128)(2,1)} %bitcast.133), channel_id=1, source_target_pairs={{0,32},{32,64},{64,96},{96,128},{128,160},{160,192},{192,224},{1,3... | collective-permute-start | bytes 1966088 | tf_op jit(solution)/shard_map/ppermute | solution.py:16
  96.2 20.3 %collective-permute-start.10 = (bf16[80,640]{1,0:T(8,128)(2,1)S(1)}, bf16[80,640]{1,0:T(8,128)(2,1)}, u32[]{:S(2)}, u32[]{:S(2)}) collective-permute-start(bf16[80,640]{1,0:T(8,128)(2,1)S(1)} %get-tuple-element.175), channel_id=1, source_target_pairs={{0,4},{2,6},{4,8},{6,10},{8,12},{10,14},{12,16},{14,18},{16,20},{1... | collective-permute-start | bytes 307208 | tf_op jit(solution)/shard_map/ppermute | solution.py:29
  98.0 18.5 %collective-permute-start.9 = (bf16[80,640]{1,0:T(8,128)(2,1)S(1)}, bf16[80,640]{1,0:T(8,128)(2,1)}, u32[]{:S(2)}, u32[]{:S(2)}) collective-permute-start(bf16[80,640]{1,0:T(8,128)(2,1)S(1)} %get-tuple-element.176), channel_id=1, source_target_pairs={{0,28},{2,30},{4,0},{6,2},{8,4},{10,6},{12,8},{14,10},{16,12},{18,... | collective-permute-start | bytes 307208 | tf_op jit(solution)/shard_map/ppermute | solution.py:29
  102.3 14.7 %collective-permute-start.11 = (bf16[80,640]{1,0:T(8,128)(2,1)}, bf16[80,640]{1,0:T(8,128)(2,1)S(1)}, u32[]{:S(2)}, u32[]{:S(2)}) collective-permute-start(bf16[80,640]{1,0:T(8,128)(2,1)} %get-tuple-element.174), channel_id=1, source_target_pairs={{0,28},{2,30},{4,0},{6,2},{8,4},{10,6},{12,8},{14,10},{16,12},{18,... | collective-permute-start | bytes 307208 | tf_op jit(solution)/shard_map/ppermute | solution.py:29
  104.1 14.1 %collective-permute-start.12 = (bf16[80,640]{1,0:T(8,128)(2,1)S(1)}, bf16[80,640]{1,0:T(8,128)(2,1)S(1)}, u32[]{:S(2)}, u32[]{:S(2)}) collective-permute-start(bf16[80,640]{1,0:T(8,128)(2,1)S(1)} %get-tuple-element.173), channel_id=1, source_target_pairs={{0,4},{2,6},{4,8},{6,10},{8,12},{10,14},{12,16},{14,18},{16,20},{1... | collective-permute-start | bytes 307208 | tf_op jit(solution)/shard_map/ppermute | solution.py:29
  118.1 63.0 %all-to-all-start.2 = ((bf16[16,2,16,1280]{3,2,1,0:T(8,128)(2,1)}), bf16[16,2,16,1280]{3,2,1,0:T(8,128)(2,1)S(1)}, u32[]{:S(2)}, u32[]{:S(2)}) async-start(bf16[16,2,16,1280]{3,2,1,0:T(8,128)(2,1)} %bitcast.25), calls=%async_computation.2 | async-start | bytes 2621440 | tf_op jit(solution)/shard_map/all_to_all | solution.py:347
  123.0 46.4 %collective-permute-start.21 = (bf16[16,16,1280]{2,1,0:T(8,128)(2,1)S(1)}, bf16[16,16,1280]{2,1,0:T(8,128)(2,1)S(1)}, u32[]{:S(2)}, u32[]{:S(2)}) collective-permute-start(bf16[16,16,1280]{2,1,0:T(8,128)(2,1)S(1)} %shard_map.94), channel_id=1, source_target_pairs={{32,0},{64,32},{96,64},{128,96},{160,128},{192,160},{224,192},{33,... | collective-permute-start | bytes 1966088 | tf_op jit(solution)/shard_map/ppermute | solution.py:16
  129.6 30.5 %collective-permute-start.16 = (bf16[80,1280]{1,0:T(8,128)(2,1)S(1)}, bf16[80,1280]{1,0:T(8,128)(2,1)S(1)}, u32[]{:S(2)}, u32[]{:S(2)}) collective-permute-start(bf16[80,1280]{1,0:T(8,128)(2,1)S(1)} %get-tuple-element.168), channel_id=1, source_target_pairs={{0,4},{2,6},{4,8},{6,10},{8,12},{10,14},{12,16},{14,18},{16,20},{1... | collective-permute-start | bytes 614408 | tf_op jit(solution)/shard_map/ppermute | solution.py:29
  131.5 27.5 %collective-permute-start.15 = (bf16[80,1280]{1,0:T(8,128)(2,1)S(1)}, bf16[80,1280]{1,0:T(8,128)(2,1)S(1)}, u32[]{:S(2)}, u32[]{:S(2)}) collective-permute-start(bf16[80,1280]{1,0:T(8,128)(2,1)S(1)} %get-tuple-element.167), channel_id=1, source_target_pairs={{0,28},{2,30},{4,0},{6,2},{8,4},{10,6},{12,8},{14,10},{16,12},{18,... | collective-permute-start | bytes 614408 | tf_op jit(solution)/shard_map/ppermute | solution.py:29
  134.3 28.6 %collective-permute-start.13 = (bf16[80,1280]{1,0:T(8,128)(2,1)S(1)}, bf16[80,1280]{1,0:T(8,128)(2,1)S(1)}, u32[]{:S(2)}, u32[]{:S(2)}) collective-permute-start(bf16[80,1280]{1,0:T(8,128)(2,1)S(1)} %get-tuple-element.170), channel_id=1, source_target_pairs={{0,28},{2,30},{4,0},{6,2},{8,4},{10,6},{12,8},{14,10},{16,12},{18,... | collective-permute-start | bytes 614408 | tf_op jit(solution)/shard_map/ppermute | solution.py:29
  136.1 27.9 %collective-permute-start.14 = (bf16[80,1280]{1,0:T(8,128)(2,1)S(1)}, bf16[80,1280]{1,0:T(8,128)(2,1)S(1)}, u32[]{:S(2)}, u32[]{:S(2)}) collective-permute-start(bf16[80,1280]{1,0:T(8,128)(2,1)S(1)} %get-tuple-element.169), channel_id=1, source_target_pairs={{0,4},{2,6},{4,8},{6,10},{8,12},{10,14},{12,16},{14,18},{16,20},{1... | collective-permute-start | bytes 614408 | tf_op jit(solution)/shard_map/ppermute | solution.py:29
  161.3 10.7 %collective-permute-start.20 = (bf16[80,1280]{1,0:T(8,128)(2,1)S(1)}, bf16[80,1280]{1,0:T(8,128)(2,1)S(1)}, u32[]{:S(2)}, u32[]{:S(2)}) collective-permute-start(bf16[80,1280]{1,0:T(8,128)(2,1)S(1)} %get-tuple-element.164), channel_id=1, source_target_pairs={{0,4},{2,6},{4,8},{6,10},{8,12},{10,14},{12,16},{14,18},{16,20},{1... | collective-permute-start | bytes 614408 | tf_op jit(solution)/shard_map/ppermute | solution.py:29
  168.8 8.4 %collective-permute-start.18 = (bf16[80,1280]{1,0:T(8,128)(2,1)S(1)}, bf16[80,1280]{1,0:T(8,128)(2,1)S(1)}, u32[]{:S(2)}, u32[]{:S(2)}) collective-permute-start(bf16[80,1280]{1,0:T(8,128)(2,1)S(1)} %get-tuple-element.165), channel_id=1, source_target_pairs={{0,4},{2,6},{4,8},{6,10},{8,12},{10,14},{12,16},{14,18},{16,20},{1... | collective-permute-start | bytes 614408 | tf_op jit(solution)/shard_map/ppermute | solution.py:29
  173.2 10.9 %collective-permute-start.23 = (bf16[80,1280]{1,0:T(8,128)(2,1)S(1)}, bf16[80,1280]{1,0:T(8,128)(2,1)S(1)}, u32[]{:S(2)}, u32[]{:S(2)}) collective-permute-start(bf16[80,1280]{1,0:T(8,128)(2,1)S(1)} %get-tuple-element.162), channel_id=1, source_target_pairs={{0,4},{2,6},{4,8},{6,10},{8,12},{10,14},{12,16},{14,18},{16,20},{1... | collective-permute-start | bytes 614408 | tf_op jit(solution)/shard_map/ppermute | solution.py:29
  (16 other events, 145.1 us)
